TPU v7x, 512 devices: a whole 4x8x8 slice. The times are simulated.
512 devices in a mesh: req: 32 (over z, x), tp: 16 (over y, core).
Axes of the slice: x: 4, y: 8, z: 8, core: 2. Of those that a mesh axis runs over, the one named last changes fastest.
Arguments:
- tokens: bfloat16 [8192, 8192], P('req', 'tp'), may hold values from -6 to 6
- w_inner: bfloat16 [8192, 8192], P('req', 'tp'), may hold values from -0.0625 to 0.0625
- w_bc: bfloat16 [8192, 32], replicated, may hold values from -0.0625 to 0.0625
- w_dt_down: bfloat16 [8192, 512], P(None, 'tp'), may hold values from -0.0625 to 0.0625
- w_dt_up: bfloat16 [512, 8192], P(None, 'tp'), may hold values from -0.25 to 0.25
- step_bias: float32 [8192], P('tp'), may hold values from -4 to 0
- decay_rate: float32 [16, 8192], P(None, 'tp'), may hold values from 0.01 to 4
- skip_gain: float32 [8192], P('tp'), may hold values from 0.5 to 1.5
- norm_gain: float32 [8192], P('tp'), may hold values from 0.5 to 1.5
- cache: float32 [32, 16, 16, 8192], P('req', None, None, 'tp'), may hold values from -6 to 6
- hits: int32 [32, 2], replicated, may hold values from 0 to 31, as said below
Outputs:
- normed: bfloat16 [8192, 8192], P('req', 'tp')
- last_state: float32 [32, 16, 8192], P('req', None, 'tp')
Inputs may be any that keep to these rules, and one draw needn't show every extreme that they name: hits[r, 0] is an index of req in 0 to 32 - 1 and hits[r, 1] a prefix length of 1 to 16 blocks; some request has 16 blocks, some prefix is held by index 0 and some by the last index of req.
All inputs are finite; a program needn't handle non-finite values.
Results may differ from a plain program's by a relative error of at most 0.0055.
Values may be sent and summed in bfloat16 or wider, within the bound.
No kernel may reach another device: no remote copies, remote signals or barrier semaphores. Data moves between devices by JAX's collectives and lax.ppermute only.
A program may use at most 64 MiB of HBM per device.

v0:
```python
import math

import jax
import jax.numpy as jnp
from jax import lax
from jax.sharding import PartitionSpec as P


def per_device(
    tokens,
    w_inner,
    w_bc,
    w_dt_down,
    w_dt_up,
    step_bias,
    decay_rate,
    skip_gain,
    norm_gain,
    cache,
    hits,
):
    whole = lax.all_gather(tokens, "tp", axis=1, tiled=True)
    rows = whole.shape[0]
    width = w_inner.shape[1]
    full_weight = lax.all_gather(w_inner, "req", axis=0, tiled=True)
    projected = jnp.dot(whole, full_weight, preferred_element_type=jnp.float32)
    inner = jax.nn.silu(projected).astype(jnp.bfloat16)
    maps = jnp.dot(whole, w_bc, preferred_element_type=jnp.float32)
    state_size = maps.shape[1] // 2
    in_map = maps[:, :state_size]
    out_map = maps[:, state_size:]
    low_part = jnp.dot(whole, w_dt_down, preferred_element_type=jnp.float32).astype(jnp.bfloat16)
    low = lax.all_gather(low_part, "tp", axis=1, tiled=True)
    step = jax.nn.softplus(
        jnp.dot(low, w_dt_up, preferred_element_type=jnp.float32) + step_bias[None, :]
    )
    here = lax.axis_index("req")
    owner = hits[:, 0]
    length = hits[:, 1]
    slots = cache.shape[1]
    picked = (length[:, None] - 1 == jnp.arange(slots, dtype=jnp.int32)[None, :]) & (owner == here)[
        :, None
    ]
    send = jnp.einsum(
        "rm,mne->rne", picked.astype(jnp.float32), cache[0], precision=lax.Precision.HIGHEST
    )
    arrived = lax.all_to_all(send, "req", split_axis=0, concat_axis=0, tiled=True)
    start = jnp.sum(arrived, axis=0)
    block = math.gcd(rows, 16)
    count = rows // block
    values_all = inner.astype(jnp.float32).reshape(count, block, width)
    ins_all = in_map.reshape(count, block, state_size)
    outs_all = out_map.reshape(count, block, state_size)
    steps_all = step.reshape(count, block, width)

    def advance(state, item):
        values, bvec, cvec, delta = item
        produced = []
        for position in range(block):
            factor = jnp.exp(-decay_rate * delta[position][None, :])
            state = (
                factor * state
                + bvec[position][:, None] * (delta[position] * values[position])[None, :]
            )
            produced.append(
                jnp.sum(cvec[position][:, None] * state, axis=0) + skip_gain * values[position]
            )
        return (state, jnp.stack(produced, axis=0))

    state, results = lax.scan(advance, start, (values_all, ins_all, outs_all, steps_all))
    out = results.reshape(rows, width)
    squares = lax.psum(jnp.sum(out * out, axis=1), "tp")
    total_width = width * lax.axis_size("tp")
    scale = lax.rsqrt(squares / total_width + 1e-05)
    normed = (out * scale[:, None] * norm_gain[None, :]).astype(jnp.bfloat16)
    return (normed, state.reshape(1, state_size, width))


def solution(mesh):
    placed = (
        P("req", "tp"),
        P("req", "tp"),
        P(),
        P(None, "tp"),
        P(None, "tp"),
        P("tp"),
        P(None, "tp"),
        P("tp"),
        P("tp"),
        P("req", None, None, "tp"),
        P(),
    )
    return jax.shard_map(
        per_device,
        mesh=mesh,
        in_specs=placed,
        out_specs=(P("req", "tp"), P("req", None, "tp")),
        check_vma=False,
    )
```

profile of v0, /device:TPU:1, one launch (start us, length us, event | category | flops | bytes accessed | tf_op | source)
XLA Modules:
  0.0 229.1 jit_solution(1960219788333433748)
XLA Ops:
  7.2 0.7 all-gather.3.cloned.1.call-update
  8.0 0.7 all-gather.5.cloned.1.call-update
  8.7 0.7 add_bitcast_fusion
  9.4 0.7 compare_bitcast_fusion
  10.1 0.8 fusion.50
  10.9 1.7 copy.17
  12.6 13.8 %all-to-all-start = ((f32[32,16,512]{2,1,0:T(8,128)}), f32[32,16,512]{2,1,0:T(8,128)S(1)}, u32[]{:S(2)}, u32[]{:S(2)}) async-start(f32[32,16,512]{2,1,0:T(8,128)} %copy.17), calls=%async_computation | async-start | bytes 2097152 | tf_op jit(solution)/shard_map/all_to_all | solution.py:47
  26.4 26.2 %all-to-all-done = f32[32,16,512]{2,1,0:T(8,128)S(1)} async-done(((f32[32,16,512]{2,1,0:T(8,128)}), f32[32,16,512]{2,1,0:T(8,128)S(1)}, u32[]{:S(2)}, u32[]{:S(2)}) %all-to-all-start) | async-done | bytes 1048608 | tf_op jit(solution)/shard_map/all_to_all | solution.py:47
  52.7 8.2 %all-gather.3.cloned.1.call-done = bf16[256,8192]{1,0:T(8,128)(2,1)} async-done(((bf16[256,512]{1,0:T(8,128)(2,1)}), bf16[256,8192]{1,0:T(8,128)(2,1)}) %all-gather.3.cloned.1.call-update) | async-done | bytes 4194320 | tf_op jit(solution)/shard_map/all_gather | solution.py:22
  60.9 3.5 %fusion.58 = f32[256,32]{0,1:T(8,128)S(1)} fusion(bf16[256,8192]{1,0:T(8,128)(2,1)} %all-gather.3.cloned.1.call-done, bf16[8192,32]{0,1:T(8,128)(2,1)S(1)} %copy-done.2), kind=kOutput, calls=%fused_computation.180 | convolution fusion | flops 134217728 | bytes 4751360 | tf_op jit(solution)/shard_map/dot_general | solution.py:28
  64.7 3.5 %convolution_convert_fusion = bf16[256,32]{0,1:T(8,128)(2,1)S(1)} fusion(bf16[256,8192]{1,0:T(8,128)(2,1)} %all-gather.3.cloned.1.call-done, bf16[8192,32]{0,1:T(8,128)(2,1)S(1)} %copy-done.3), kind=kOutput, calls=%fused_computation.163 | convolution fusion | flops 134225920 | bytes 4734976 | tf_op jit(solution)/shard_map/dot_general | solution.py:32
  68.2 16.8 %all_gather.10 = bf16[256,512]{0,1:T(8,128)(2,1)S(1)} all-gather(bf16[256,32]{0,1:T(8,128)(2,1)S(1)} %convolution_convert_fusion), channel_id=1, replica_groups=mesh['req'=32,'tp'=16] {'tp'}, dimensions={1}, use_global_device_ids=true | all-gather | bytes 278528 | tf_op jit(solution)/shard_map/all_gather | solution.py:33
  85.0 0.5 compare_select_fusion
  85.6 81.2 %all-gather.5.cloned.1.call-done = bf16[8192,512]{1,0:T(8,128)(2,1)} async-done(((bf16[256,512]{1,0:T(8,128)(2,1)}), bf16[8192,512]{1,0:T(8,128)(2,1)}) %all-gather.5.cloned.1.call-update) | async-done | bytes 8388624 | tf_op jit(solution)/shard_map/all_gather | solution.py:25
  166.8 7.1 %multiply_convert_fusion = bf16[256,512]{1,0:T(8,128)(2,1)S(1)} fusion(bf16[256,8192]{1,0:T(8,128)(2,1)} %all-gather.3.cloned.1.call-done, bf16[8192,512]{1,0:T(8,128)(2,1)} %all-gather.5.cloned.1.call-done), kind=kOutput, calls=%fused_computation.170 | convolution fusion | flops 2148139008 | bytes 12845056 | tf_op jit(solution)/shard_map/dot_general | solution.py:26
  174.0 23.3 %while.14 = (s32[]{:T(128)}, f32[16,512]{1,0:T(8,128)S(1)}, f32[16,16,512]{2,1,0:T(8,128)S(1)}, f32[16,16,512]{2,1,0:T(8,128)S(1)}, f32[16,512]{1,0:T(8,128)S(1)...) while((s32[]{:T(128)}, f32[16,512]{1,0:T(8,128)S(1)}, ...), condition=%wide.region_18.19_spmd, body=%wide.region_1.18_spmd.sunk | while | flops 1196049 | bytes 1076517 | solution.py:70
  174.7 0.2 multiply_reduce_fusion.22
  176.1 0.2 multiply_reduce_fusion.22
  179.0 0.2 multiply_reduce_fusion.22
  180.5 0.2 multiply_reduce_fusion.22
  181.9 0.2 multiply_reduce_fusion.22
  183.4 0.2 multiply_reduce_fusion.22
  197.5 24.0 %psum.7 = f32[256]{0:T(256)S(1)} all-reduce(f32[256]{0:T(256)S(1)} %reduce_sum.230), channel_id=1, replica_groups=mesh['req'=32,'tp'=16] {'tp'}, use_global_device_ids=true, to_apply=%region_20.21 | all-reduce | flops 256 | bytes 2048 | tf_op jit(solution)/shard_map/psum | solution.py:72
  221.5 0.8 fusion.49
  (456 shorter events, 19.7 us)
Async XLA Ops:
  7.2 2.9 %copy-start = (f32[1,16,16,512]{3,2,1,0:T(8,128)S(1)}, f32[1,16,16,512]{3,2,1,0:T(8,128)}, u32[]{:S(2)}) copy-start(f32[1,16,16,512]{3,2,1,0:T(8,128)} %param.22) | copy-start | bytes 1572868
  7.2 19.2 %copy-start.5 = (f32[16,512]{1,0:T(8,128)S(1)}, f32[16,512]{1,0:T(8,128)}, u32[]{:S(2)}) copy-start(f32[16,512]{1,0:T(8,128)} %param.19) | copy-start | bytes 98308
  7.2 53.7 %copy-start.2 = (bf16[8192,32]{0,1:T(8,128)(2,1)S(1)}, bf16[8192,32]{0,1:T(8,128)(2,1)}, u32[]{:S(2)}) copy-start(bf16[8192,32]{0,1:T(8,128)(2,1)} %param.15) | copy-start | bytes 1572868
  7.2 53.7 %all-gather.3.cloned.1.call-start = ((), (), s32[]{:S(2)}) async-start(), calls=%async_computation.1 | async-start | bytes 4456448 | tf_op jit(solution)/shard_map/all_gather | solution.py:22
  7.9 158.9 %all-gather.5.cloned.1.call-start = ((), (), s32[]{:S(2)}) async-start(), calls=%async_computation.2 | async-start | bytes 8650752 | tf_op jit(solution)/shard_map/all_gather | solution.py:25
  12.6 52.1 %copy-start.3 = (bf16[8192,32]{0,1:T(8,128)(2,1)S(1)}, bf16[8192,32]{0,1:T(8,128)(2,1)}, u32[]{:S(2)}) copy-start(bf16[8192,32]{0,1:T(8,128)(2,1)} %param.16) | copy-start | bytes 1572868
  12.6 40.1 %all-to-all-start = ((f32[32,16,512]{2,1,0:T(8,128)}), f32[32,16,512]{2,1,0:T(8,128)S(1)}, u32[]{:S(2)}, u32[]{:S(2)}) async-start(f32[32,16,512]{2,1,0:T(8,128)} %copy.17), calls=%async_computation | async-start | bytes 2097152 | tf_op jit(solution)/shard_map/all_to_all | solution.py:47
  52.7 32.3 %copy-start.7 = (bf16[512,512]{1,0:T(8,128)(2,1)S(1)}, bf16[512,512]{1,0:T(8,128)(2,1)}, u32[]{:S(2)}) copy-start(bf16[512,512]{1,0:T(8,128)(2,1)} %param.17) | copy-start | bytes 1572868
  52.7 32.3 %copy-start.8 = (f32[512]{0:T(512)S(1)}, f32[512]{0:T(512)}, u32[]{:S(2)}) copy-start(f32[512]{0:T(512)} %param.18) | copy-start | bytes 6148
  85.6 88.4 %copy-start.4 = (f32[512]{0:T(512)S(1)}, f32[512]{0:T(512)}, u32[]{:S(2)}) copy-start(f32[512]{0:T(512)} %param.20) | copy-start | bytes 6148
  174.0 47.5 %copy-start.6 = (f32[512]{0:T(512)S(1)}, f32[512]{0:T(512)}, u32[]{:S(2)}) copy-start(f32[512]{0:T(512)} %param.21) | copy-start | bytes 6148
  197.3 25.0 %copy-start.1 = (f32[16,512]{1,0:T(8,128)}, f32[16,512]{1,0:T(8,128)S(1)}, u32[]{:S(2)}) copy-start(f32[16,512]{1,0:T(8,128)S(1)} %get-tuple-element.109) | copy-start | bytes 98308
Sparse Core Ops, SparseCore 0:
  10.2 50.6 all-gather.2
  64.1 102.7 all-gather.4
where the time goes:
time: 229 us
  waiting for transfers between devices  117 us (51%)
  blocking collectives  40.8 us (18%)
  other arithmetic  15.8 us (7%)
  matrix products  15.5 us (7%)
  between operations  14.2 us (6%)
  starting transfers between devices  13.9 us (6%)
  local copies, waits for them, and re-layouts  9.17 us (4%)
  loops' own time  2.77 us (1%)
    all_gather x1, waiting for transfers between devices, per_device(): full_weight = lax.all_gather(w_inner, 'req', axis=0, tiled=True)  81.2 us
    all_to_all x1, waiting for transfers between devices, per_device(): lax.all_to_all(send, 'req', split_axis=0, concat_axis=0, tiled=True)  26.2 us
    psum x1, blocking collectives, per_device(): squares = lax.psum(jnp.sum(out * out, axis=1), 'tp')  24 us
    all_gather x1, blocking collectives, per_device(): low = lax.all_gather(low_part, 'tp', axis=1, tiled=True)  16.8 us
    all_to_all x1, starting transfers between devices, per_device(): lax.all_to_all(send, 'req', split_axis=0, concat_axis=0, tiled=True)  13.8 us
    reduce_sum x80, other arithmetic, advance(): jnp.sum(cvec[position][:, None] * state, axis=0)  11.3 us
    all_gather x1, waiting for transfers between devices, per_device(): whole = lax.all_gather(tokens, 'tp', axis=1, tiled=True)  8.18 us
    dot_general x1, matrix products, per_device(): projected = jnp.dot(whole, full_weight, preferred_element_type=jnp.float32)  7.06 us
  transfers between devices with their start and end apart: 3, of which 3 were waited for; matrix products, arithmetic and copies ran while one was open for 5% of the time, Pallas kernels for 0%

commit v1 on v0

v1 whole, which is shorter than its diff:
```python
import jax
import jax.numpy as jnp
from jax import lax
from jax.experimental import pallas as pl
from jax.experimental.pallas import tpu as pltpu
from jax.sharding import PartitionSpec as P

LOG2E = 1.4426950408889634
GROUP = 8


def scan_kernel(values, steps, ins, outs, decay, skip, start, out, state, squares):
    rows, width = out.shape
    rate = decay[...] * -LOG2E
    gain = skip[...]
    line = lax.broadcasted_iota(jnp.int32, (GROUP, width), 0)

    def merge(low, high, bit):
        upper = (line & bit) != 0
        kept = jnp.where(upper, high, low)
        moved = jnp.where(upper, low, high)
        return kept + pltpu.roll(moved, GROUP - bit, 0)

    def advance(index, held):
        first = pl.multiple_of(index * GROUP, GROUP)
        value = values[pl.ds(first, GROUP), :].astype(jnp.float32)
        step = steps[pl.ds(first, GROUP), :]
        fed = step * value
        terms = []
        for at in range(GROUP):
            factor = jnp.exp2(rate * step[at : at + 1, :])
            into = jnp.tile(ins[first + at], (1, width // 128))
            held = factor * held + into * fed[at : at + 1, :]
            onto = jnp.tile(outs[first + at], (1, width // 128)) * held
            terms.append(onto[:GROUP] + onto[GROUP:])
        for bit in (1, 2, 4):
            terms = [merge(low, high, bit) for low, high in zip(terms[::2], terms[1::2])]
        out[pl.ds(first, GROUP), :] = terms[0] + gain * value
        return held

    state[...] = lax.fori_loop(0, rows // GROUP, advance, start[...].astype(jnp.float32))
    whole = out[...]
    ones = jnp.ones((squares.shape[0], width), jnp.float32)
    squares[...] = lax.dot_general(
        ones,
        whole * whole,
        (((1,), (1,)), ((), ())),
        precision=lax.Precision.HIGHEST,
        preferred_element_type=jnp.float32,
    )


def run_scan(values, steps, ins, outs, decay, skip, start, copies):
    rows, width = values.shape
    cells = rows * width * decay.shape[0]
    return pl.pallas_call(
        scan_kernel,
        out_shape=(
            jax.ShapeDtypeStruct((rows, width), jnp.float32),
            jax.ShapeDtypeStruct(decay.shape, jnp.float32),
            jax.ShapeDtypeStruct((copies, rows), jnp.float32),
        ),
        compiler_params=pltpu.CompilerParams(vmem_limit_bytes=32 * 1024 * 1024),
        cost_estimate=pl.CostEstimate(flops=8 * cells, bytes_accessed=8 << 20, transcendentals=cells),
    )(values, steps, ins, outs, decay, skip, start)


def ring(block, axis, forward, backward, turns):
    half = block.shape[0] // 2
    after, before = [block], []
    left = right = block
    for _ in range(turns // 2 - 1):
        left = lax.ppermute(left, axis, forward)
        right = lax.ppermute(right, axis, backward)
        after.append(left)
        before.append(right)
    far = jnp.concatenate(
        [lax.ppermute(left[:half], axis, forward), lax.ppermute(right[half:], axis, backward)], axis=0
    )
    return jnp.stack(after + [far] + before[::-1], axis=0)


def per_device(
    tokens,
    w_inner,
    w_bc,
    w_dt_down,
    w_dt_up,
    step_bias,
    decay_rate,
    skip_gain,
    norm_gain,
    cache,
    hits,
):
    rows, share = tokens.shape
    width = w_inner.shape[1]
    parts = lax.axis_size("tp")
    chips = parts // 2
    place = lax.axis_index("tp")
    full_weight = lax.all_gather(w_inner, "req", axis=0, tiled=True)

    up = [(2 * y + c, 2 * ((y + 1) % chips) + c) for y in range(chips) for c in range(2)]
    down = [(b, a) for a, b in up]
    swap = [(i, i ^ 1) for i in range(parts)]
    mine = ring(tokens, "tp", up, down, chips)
    other = lax.ppermute(mine, "tp", swap)
    core = place % 2
    pair = jnp.where(
        core == 0, jnp.stack([mine, other], axis=1), jnp.stack([other, mine], axis=1)
    )
    order = (place // 2 - jnp.arange(chips)) % chips
    whole = jnp.transpose(jnp.take(pair, order, axis=0), (2, 0, 1, 3)).reshape(rows, parts * share)

    here = lax.axis_index("req")
    states = jnp.take(cache[0].astype(jnp.bfloat16), hits[:, 1] - 1, axis=0)
    arrived = lax.all_to_all(states, "req", split_axis=0, concat_axis=0, tiled=True)
    start = lax.dynamic_index_in_dim(arrived, hits[here, 0], axis=0, keepdims=False)

    state_size = decay_rate.shape[0]
    maps = jnp.dot(whole, w_bc, preferred_element_type=jnp.float32)
    spread = jnp.broadcast_to(maps[:, :, None], (rows, 2 * state_size, 128))
    low_part = jnp.dot(whole, w_dt_down, preferred_element_type=jnp.float32).astype(jnp.bfloat16)
    low = lax.all_gather(low_part, "tp", axis=1, tiled=True)
    step = jax.nn.softplus(
        jnp.dot(low, w_dt_up, preferred_element_type=jnp.float32) + step_bias[None, :]
    )

    projected = jnp.dot(whole, full_weight, preferred_element_type=jnp.float32)
    inner = jax.nn.silu(projected).astype(jnp.bfloat16)
    out, state, squares = run_scan(
        inner,
        step,
        spread[:, :state_size],
        spread[:, state_size:],
        decay_rate,
        skip_gain[None, :],
        start,
        parts,
    )
    sums = jnp.sum(lax.all_to_all(squares, "tp", split_axis=0, concat_axis=0, tiled=True), axis=0)
    scale = lax.rsqrt(sums / (width * parts) + 1e-05)
    normed = (out * scale[:, None] * norm_gain[None, :]).astype(jnp.bfloat16)
    return (normed, state.reshape(1, state_size, width))


def solution(mesh):
    placed = (
        P("req", "tp"),
        P("req", "tp"),
        P(),
        P(None, "tp"),
        P(None, "tp"),
        P("tp"),
        P(None, "tp"),
        P("tp"),
        P("tp"),
        P("req", None, None, "tp"),
        P(),
    )
    return jax.shard_map(
        per_device,
        mesh=mesh,
        in_specs=placed,
        out_specs=(P("req", "tp"), P("req", None, "tp")),
        check_vma=False,
    )
```

time: 229 us -> 174 us (0.76)
  waiting for transfers between devices: 117 us -> 34 us
  starting transfers between devices: 13.9 us -> 49.7 us
  blocking collectives: 40.8 us -> 29.2 us
  local copies, waits for them, and re-layouts: 9.17 us -> 15.3 us
  other arithmetic: 15.8 us -> 11.2 us
  Pallas kernels: 0 us -> 3.81 us
  loops' own time: 2.77 us -> 0 us
    all_gather x1, waiting for transfers between devices: 81.2 us -> 0.02 us  [per_device(): full_weight = lax.all_gather(w_inner, 'req', axis=0, tiled=True)]
    ppermute x0 -> x9, starting transfers between devices: none -> 41.3 us  [the longest x3 13 us: ring(): right = lax.ppermute(right, axis, backward)]
    psum x1 -> x0, blocking collectives: 24 us -> none  [per_device(): squares = lax.psum(jnp.sum(out * out, axis=1), 'tp')]
    all_to_all x0 -> x1, blocking collectives: none -> 13.9 us  [per_device(): lax.all_to_all(squares, 'tp', split_axis=0, concat_axis=0, tiled=True)]
    ppermute x0 -> x9, waiting for transfers between devices: none -> 12.6 us  [the longest x3 4.41 us: ring(): right = lax.ppermute(right, axis, backward)]
    reduce_sum x82 -> x1, other arithmetic: 11.5 us -> 0.04 us  [per_device(): jnp.sum(lax.all_to_all(squares, 'tp', split_axis=0, concat_axis=0, tiled=...]
    select_n x0 -> x5, other arithmetic: none -> 10.2 us  [the longest x2 4.7 us: per_device(): jnp.take(pair, order, axis=0)]
    all_gather x1 -> x0, waiting for transfers between devices: 8.18 us -> none  [per_device(): whole = lax.all_gather(tokens, 'tp', axis=1, tiled=True)]
  transfers between devices with their start and end apart: 3 -> 11, of which waited for: 3 -> 6; matrix products, arithmetic and copies ran while one was open for 5% -> 18% of each run, Pallas kernels for 0% -> 0%
where the time goes in v1:
time: 174 us; the launch traced here: 173 us
  starting transfers between devices  49.7 us (29%)
  waiting for transfers between devices  34 us (20%)
  blocking collectives  29.2 us (17%)
  between operations  16.4 us (9%)
  local copies, waits for them, and re-layouts  15.3 us (9%)
  matrix products  13.8 us (8%)
  other arithmetic  11.2 us (6%)
  Pallas kernels  3.81 us (2%)
    all_to_all x1, waiting for transfers between devices, per_device(): lax.all_to_all(states, 'req', split_axis=0, concat_axis=0, tiled=True)  20.7 us
    all_gather x1, blocking collectives, per_device(): low = lax.all_gather(low_part, 'tp', axis=1, tiled=True)  15.3 us
    all_to_all x1, blocking collectives, per_device(): lax.all_to_all(squares, 'tp', split_axis=0, concat_axis=0, tiled=True)  13.9 us
    ppermute x3, starting transfers between devices, ring(): right = lax.ppermute(right, axis, backward)  13 us
    ppermute x1, starting transfers between devices, per_device(): other = lax.ppermute(mine, 'tp', swap)  12.4 us
    ppermute x3, starting transfers between devices, ring(): left = lax.ppermute(left, axis, forward)  8.55 us
    all_to_all x1, starting transfers between devices, per_device(): lax.all_to_all(states, 'req', split_axis=0, concat_axis=0, tiled=True)  8.34 us
    dot_general x1, matrix products, per_device(): projected = jnp.dot(whole, full_weight, preferred_element_type=jnp.float32)  7.08 us
  transfers between devices with their start and end apart: 11, of which 6 were waited for; matrix products, arithmetic and copies ran while one was open for 18% of the time, Pallas kernels for 0%

profile of v1, /device:TPU:1, one launch (start us, length us, event | category | flops | bytes accessed | tf_op | source)
XLA Modules:
  0.0 173.3 jit_solution(14242271520159647393)
XLA Ops:
  7.9 4.0 %collective-permute-start = (bf16[256,512]{1,0:T(8,128)(2,1)}, bf16[256,512]{1,0:T(8,128)(2,1)S(1)}, u32[]{:S(2)}, u32[]{:S(2)}) collective-permute-start(bf16[256,512]{1,0:T(8,128)(2,1)} %param.11), channel_id=1, source_target_pairs={{0,2},{1,3},{2,4},{3,5},{4,6},{5,7},{6,8},{7,9},{8,10},{9,11},{10,... | collective-permute-start | bytes 786440 | tf_op jit(solution)/shard_map/ppermute | solution.py:73
  12.0 3.8 %collective-permute-start.4 = (bf16[256,512]{1,0:T(8,128)(2,1)}, bf16[256,512]{1,0:T(8,128)(2,1)S(1)}, u32[]{:S(2)}, u32[]{:S(2)}) collective-permute-start(bf16[256,512]{1,0:T(8,128)(2,1)} %param.11), channel_id=1, source_target_pairs={{2,0},{3,1},{4,2},{5,3},{6,4},{7,5},{8,6},{9,7},{10,8},{11,9},{12,... | collective-permute-start | bytes 786440 | tf_op jit(solution)/shard_map/ppermute | solution.py:74
  15.8 2.0 %collective-permute-done = bf16[256,512]{1,0:T(8,128)(2,1)S(1)} collective-permute-done((bf16[256,512]{1,0:T(8,128)(2,1)}, bf16[256,512]{1,0:T(8,128)(2,1)S(1)}, u32[]{:S(2)}, u32[]{:S(2)}) %collective-permute-start) | collective-permute-done | bytes 262176 | tf_op jit(solution)/shard_map/ppermute | solution.py:73
  17.8 2.6 %collective-permute-start.1 = (bf16[256,512]{1,0:T(8,128)(2,1)S(1)}, bf16[256,512]{1,0:T(8,128)(2,1)S(1)}, u32[]{:S(2)}, u32[]{:S(2)}) collective-permute-start(bf16[256,512]{1,0:T(8,128)(2,1)S(1)} %collective-permute-done), channel_id=1, source_target_pairs={{0,2},{1,3},{2,4},{3,5},{4,6},{5,7},{6,8},{7,9},{8,10},{9,11},{10,... | collective-permute-start | bytes 786440 | tf_op jit(solution)/shard_map/ppermute | solution.py:73
  20.5 4.6 %collective-permute-start.5 = (bf16[256,512]{1,0:T(8,128)(2,1)S(1)}, bf16[256,512]{1,0:T(8,128)(2,1)S(1)}, u32[]{:S(2)}, u32[]{:S(2)}) collective-permute-start(bf16[256,512]{1,0:T(8,128)(2,1)S(1)} %collective-permute-done.4), channel_id=1, source_target_pairs={{2,0},{3,1},{4,2},{5,3},{6,4},{7,5},{8,6},{9,7},{10,8},{11,9},{12,... | collective-permute-start | bytes 786440 | tf_op jit(solution)/shard_map/ppermute | solution.py:74
  26.9 1.9 %collective-permute-start.2 = (bf16[256,512]{1,0:T(8,128)(2,1)S(1)}, bf16[256,512]{1,0:T(8,128)(2,1)S(1)}, u32[]{:S(2)}, u32[]{:S(2)}) collective-permute-start(bf16[256,512]{1,0:T(8,128)(2,1)S(1)} %collective-permute-done.1), channel_id=1, source_target_pairs={{0,2},{1,3},{2,4},{3,5},{4,6},{5,7},{6,8},{7,9},{8,10},{9,11},{10,... | collective-permute-start | bytes 786440 | tf_op jit(solution)/shard_map/ppermute | solution.py:73
  28.8 4.6 %collective-permute-start.6 = (bf16[256,512]{1,0:T(8,128)(2,1)S(1)}, bf16[256,512]{1,0:T(8,128)(2,1)S(1)}, u32[]{:S(2)}, u32[]{:S(2)}) collective-permute-start(bf16[256,512]{1,0:T(8,128)(2,1)S(1)} %collective-permute-done.5), channel_id=1, source_target_pairs={{2,0},{3,1},{4,2},{5,3},{6,4},{7,5},{8,6},{9,7},{10,8},{11,9},{12,... | collective-permute-start | bytes 786440 | tf_op jit(solution)/shard_map/ppermute | solution.py:74
  33.5 4.4 %collective-permute-done.6 = bf16[256,512]{1,0:T(8,128)(2,1)S(1)} collective-permute-done((bf16[256,512]{1,0:T(8,128)(2,1)S(1)}, bf16[256,512]{1,0:T(8,128)(2,1)S(1)}, u32[]{:S(2)}, u32[]{:S(2)}) %collective-permute-start.6) | collective-permute-done | bytes 262176 | tf_op jit(solution)/shard_map/ppermute | solution.py:74
  37.9 5.4 %collective-permute-start.7 = (bf16[128,512]{1,0:T(8,128)(2,1)S(1)}, bf16[128,512]{1,0:T(8,128)(2,1)S(1)}, u32[]{:S(2)}, u32[]{:S(2)}) collective-permute-start(bf16[128,512]{1,0:T(8,128)(2,1)S(1)} %slice.27), channel_id=1, source_target_pairs={{2,0},{3,1},{4,2},{5,3},{6,4},{7,5},{8,6},{9,7},{10,8},{11,9},{12,... | collective-permute-start | bytes 393224 | tf_op jit(solution)/shard_map/ppermute | solution.py:78
  43.3 1.9 %collective-permute-start.3 = (bf16[128,512]{1,0:T(8,128)(2,1)S(1)}, bf16[128,512]{1,0:T(8,128)(2,1)S(1)}, u32[]{:S(2)}, u32[]{:S(2)}) collective-permute-start(bf16[128,512]{1,0:T(8,128)(2,1)S(1)} %slice.26), channel_id=1, source_target_pairs={{0,2},{1,3},{2,4},{3,5},{4,6},{5,7},{6,8},{7,9},{8,10},{9,11},{10,... | collective-permute-start | bytes 393224 | tf_op jit(solution)/shard_map/ppermute | solution.py:78
  46.6 4.0 %collective-permute-done.3 = bf16[128,512]{1,0:T(8,128)(2,1)S(1)} collective-permute-done((bf16[128,512]{1,0:T(8,128)(2,1)S(1)}, bf16[128,512]{1,0:T(8,128)(2,1)S(1)}, u32[]{:S(2)}, u32[]{:S(2)}) %collective-permute-start.3) | collective-permute-done | bytes 131104 | tf_op jit(solution)/shard_map/ppermute | solution.py:78
  50.7 12.4 %collective-permute-start.8 = (bf16[8,256,512]{2,1,0:T(8,128)(2,1)S(1)}, bf16[8,256,512]{2,1,0:T(8,128)(2,1)}, u32[]{:S(2)}, u32[]{:S(2)}) collective-permute-start(bf16[8,256,512]{2,1,0:T(8,128)(2,1)S(1)} %bitcast_dynamic-update-slice_fusion), channel_id=1, source_target_pairs={{0,1},{1,0},{2,3},{3,2},{4,5},{5,4},{6,7},{7,6},{8,9},{9,8},{10,11... | collective-permute-start | bytes 6291464 | tf_op jit(solution)/shard_map/ppermute | solution.py:107
  64.8 8.3 %all-to-all-start = ((bf16[32,16,512]{2,1,0:T(8,128)(2,1)}), bf16[32,16,512]{2,1,0:T(8,128)(2,1)S(1)}, u32[]{:S(2)}, u32[]{:S(2)}) async-start(bf16[32,16,512]{2,1,0:T(8,128)(2,1)} %broadcast_select_fusion), calls=%async_computation | async-start | bytes 1048576 | tf_op jit(solution)/shard_map/all_to_all | solution.py:117
  75.8 20.7 %all-to-all-done = bf16[32,16,512]{2,1,0:T(8,128)(2,1)S(1)} async-done(((bf16[32,16,512]{2,1,0:T(8,128)(2,1)}), bf16[32,16,512]{2,1,0:T(8,128)(2,1)S(1)}, u32[]{:S(2)}, u32[]{:S(2)}) %all-to-all-start) | async-done | bytes 524320 | tf_op jit(solution)/shard_map/all_to_all | solution.py:117
  96.5 4.5 %maximum_select_fusion = bf16[8,2,256,512]{3,2,1,0:T(8,128)(2,1)} fusion(bf16[8,1,256,512]{3,2,1,0:T(8,128)(2,1)} %bitcast.9, bf16[8,1,256,512]{3,2,1,0:T(8,128)(2,1)S(1)} %bitcast.50, pred[]{:T(512)S(6)} %eq.7), kind=kLoop, calls=%fused_computation.2 | loop fusion | flops 6291456 | bytes 8388609 | tf_op jit(solution)/shard_map/jit(_where)/select_n | solution.py:109
  101.0 5.0 %gather_fusion = bf16[8,2,256,512]{3,2,1,0:T(8,128)(2,1)} fusion(bf16[8,2,256,512]{3,2,1,0:T(8,128)(2,1)} %maximum_select_fusion, s32[1024]{0:T(1024)S(1)} %pad_clamp_fusion.1), kind=kCustom, calls=%fused_computation | custom fusion | bytes 8388640 | tf_op jit(solution)/shard_map/jit(_take)/gather | solution.py:113
  106.1 4.7 %select_bitcast_fusion = bf16[256,8,2,512]{3,0,2,1:T(8,128)(2,1)} fusion(bf16[8,2,256,512]{3,2,1,0:T(8,128)(2,1)} %gather_fusion, pred[8]{0:T(512)(128)(4,1)S(1)} %compare_and_fusion), kind=kLoop, calls=%fused_computation.3 | loop fusion | flops 2097152 | bytes 8388616 | tf_op jit(solution)/shard_map/jit(_take)/select_n | solution.py:113
  110.7 6.5 %copy.20 = bf16[256,8,2,512]{0,3,2,1:T(8,128)(2,1)} copy(bf16[256,8,2,512]{3,0,2,1:T(8,128)(2,1)} %select_bitcast_fusion) | data formatting | bytes 8388608 | tf_op jit(solution)/shard_map/jit(_take)/select_n | solution.py:113
  117.3 3.1 %fusion.6 = f32[256,32]{0,1:T(8,128)S(1)} fusion(bf16[8192,32]{0,1:T(8,128)(2,1)S(1)} %copy-done.3, bf16[256,8192]{0,1:T(8,128)(2,1)} %bitcast.47), kind=kOutput, calls=%fused_computation.41 | convolution fusion | flops 134217728 | bytes 4751360 | tf_op jit(solution)/shard_map/dot_general | solution.py:121
  120.6 3.1 %convolution_convert_fusion = bf16[256,32]{0,1:T(8,128)(2,1)S(1)} fusion(bf16[8192,32]{0,1:T(8,128)(2,1)S(1)} %copy-done.4, bf16[256,8192]{0,1:T(8,128)(2,1)} %bitcast.48), kind=kOutput, calls=%fused_computation.6 | convolution fusion | flops 134225920 | bytes 4734976 | tf_op jit(solution)/shard_map/dot_general | solution.py:123
  123.6 15.3 %all_gather.7 = bf16[256,512]{0,1:T(8,128)(2,1)S(1)} all-gather(bf16[256,32]{0,1:T(8,128)(2,1)S(1)} %convolution_convert_fusion), channel_id=1, replica_groups=mesh['req'=32,'tp'=16] {'tp'}, dimensions={1}, use_global_device_ids=true | all-gather | bytes 278528 | tf_op jit(solution)/shard_map/all_gather | solution.py:124
  139.5 7.1 %multiply_convert_fusion.1.values = bf16[256,512]{1,0:T(8,128)(2,1)S(1)} fusion(bf16[256,8192]{0,1:T(8,128)(2,1)} %bitcast.49, bf16[8192,512]{1,0:T(8,128)(2,1)} %all-gather.2.cloned.1.call-done), kind=kOutput, calls=%fused_computation.8 | convolution fusion | flops 2148139008 | bytes 12845056 | tf_op jit(solution)/shard_map/dot_general | solution.py:129
  147.9 3.8 %shard_map.122 = (f32[256,512]{1,0:T(8,128)S(1)}, f32[16,512]{1,0:T(8,128)}, f32[16,256]{1,0:T(8,128)S(1)}) custom-call(bf16[256,512]{1,0:T(8,128)(2,1)S(1)} %multiply_convert_fusion.1.values, f32[256,512]{1,0:T(8,128)S(1)} %compare_select_fusion.steps, f32[256,16,128]{2,1,0:T(8,128)S(1)} %broadcast_in_dim.36.ins, ...), custom_call_target="tpu_custom_call" | custom-call | flops 16777216 | bytes 8388608 | tf_op jit(solution)/shard_map/pallas_call | solution.py:56
  151.7 13.9 %all_to_all.14 = f32[16,1,256]{2,1,0:T(1,128)S(1)} all-to-all(f32[16,1,256]{2,1,0:T(1,128)S(1)} %copy.23), channel_id=1, replica_groups=mesh['req'=32,'tp'=16] {'tp'}, dimensions={0} | all-to-all | bytes 32768 | tf_op jit(solution)/shard_map/all_to_all | solution.py:141
  (58 shorter events, 9.1 us)
Async XLA Ops:
  7.2 131.8 %copy-start = (bf16[512,512]{1,0:T(8,128)(2,1)S(1)}, bf16[512,512]{1,0:T(8,128)(2,1)}, u32[]{:S(2)}) copy-start(bf16[512,512]{1,0:T(8,128)(2,1)} %param.15) | copy-start | bytes 1572868
  7.2 56.0 %copy-start.8 = (s32[32,2]{0,1:T(2,128)S(1)}, s32[32,2]{0,1:T(2,128)}, u32[]{:S(2)}) copy-start(s32[32,2]{0,1:T(2,128)} %param.21) | copy-start | bytes 772
  7.2 56.0 %copy-start.5 = (f32[1,16,16,512]{3,2,1,0:T(8,128)S(1)}, f32[1,16,16,512]{3,2,1,0:T(8,128)}, u32[]{:S(2)}) copy-start(f32[1,16,16,512]{3,2,1,0:T(8,128)} %param.20) | copy-start | bytes 1572868
  7.2 132.3 %all-gather.2.cloned.1.call-start = ((), (), s32[]{:S(2)}) async-start(), calls=%async_computation.2 | async-start | bytes 8650752 | tf_op jit(solution)/shard_map/all_gather | solution.py:101
  7.9 9.9 %collective-permute-start = (bf16[256,512]{1,0:T(8,128)(2,1)}, bf16[256,512]{1,0:T(8,128)(2,1)S(1)}, u32[]{:S(2)}, u32[]{:S(2)}) collective-permute-start(bf16[256,512]{1,0:T(8,128)(2,1)} %param.11), channel_id=1, source_target_pairs={{0,2},{1,3},{2,4},{3,5},{4,6},{5,7},{6,8},{7,9},{8,10},{9,11},{10,... | collective-permute-start | bytes 786440 | tf_op jit(solution)/shard_map/ppermute | solution.py:73
  12.0 8.5 %collective-permute-start.4 = (bf16[256,512]{1,0:T(8,128)(2,1)}, bf16[256,512]{1,0:T(8,128)(2,1)S(1)}, u32[]{:S(2)}, u32[]{:S(2)}) collective-permute-start(bf16[256,512]{1,0:T(8,128)(2,1)} %param.11), channel_id=1, source_target_pairs={{2,0},{3,1},{4,2},{5,3},{6,4},{7,5},{8,6},{9,7},{10,8},{11,9},{12,... | collective-permute-start | bytes 786440 | tf_op jit(solution)/shard_map/ppermute | solution.py:74
  17.8 9.1 %collective-permute-start.1 = (bf16[256,512]{1,0:T(8,128)(2,1)S(1)}, bf16[256,512]{1,0:T(8,128)(2,1)S(1)}, u32[]{:S(2)}, u32[]{:S(2)}) collective-permute-start(bf16[256,512]{1,0:T(8,128)(2,1)S(1)} %collective-permute-done), channel_id=1, source_target_pairs={{0,2},{1,3},{2,4},{3,5},{4,6},{5,7},{6,8},{7,9},{8,10},{9,11},{10,... | collective-permute-start | bytes 786440 | tf_op jit(solution)/shard_map/ppermute | solution.py:73
  20.5 8.3 %collective-permute-start.5 = (bf16[256,512]{1,0:T(8,128)(2,1)S(1)}, bf16[256,512]{1,0:T(8,128)(2,1)S(1)}, u32[]{:S(2)}, u32[]{:S(2)}) collective-permute-start(bf16[256,512]{1,0:T(8,128)(2,1)S(1)} %collective-permute-done.4), channel_id=1, source_target_pairs={{2,0},{3,1},{4,2},{5,3},{6,4},{7,5},{8,6},{9,7},{10,8},{11,9},{12,... | collective-permute-start | bytes 786440 | tf_op jit(solution)/shard_map/ppermute | solution.py:74
  26.9 16.4 %collective-permute-start.2 = (bf16[256,512]{1,0:T(8,128)(2,1)S(1)}, bf16[256,512]{1,0:T(8,128)(2,1)S(1)}, u32[]{:S(2)}, u32[]{:S(2)}) collective-permute-start(bf16[256,512]{1,0:T(8,128)(2,1)S(1)} %collective-permute-done.1), channel_id=1, source_target_pairs={{0,2},{1,3},{2,4},{3,5},{4,6},{5,7},{6,8},{7,9},{8,10},{9,11},{10,... | collective-permute-start | bytes 786440 | tf_op jit(solution)/shard_map/ppermute | solution.py:73
  28.8 9.0 %collective-permute-start.6 = (bf16[256,512]{1,0:T(8,128)(2,1)S(1)}, bf16[256,512]{1,0:T(8,128)(2,1)S(1)}, u32[]{:S(2)}, u32[]{:S(2)}) collective-permute-start(bf16[256,512]{1,0:T(8,128)(2,1)S(1)} %collective-permute-done.5), channel_id=1, source_target_pairs={{2,0},{3,1},{4,2},{5,3},{6,4},{7,5},{8,6},{9,7},{10,8},{11,9},{12,... | collective-permute-start | bytes 786440 | tf_op jit(solution)/shard_map/ppermute | solution.py:74
  37.9 8.7 %collective-permute-start.7 = (bf16[128,512]{1,0:T(8,128)(2,1)S(1)}, bf16[128,512]{1,0:T(8,128)(2,1)S(1)}, u32[]{:S(2)}, u32[]{:S(2)}) collective-permute-start(bf16[128,512]{1,0:T(8,128)(2,1)S(1)} %slice.27), channel_id=1, source_target_pairs={{2,0},{3,1},{4,2},{5,3},{6,4},{7,5},{8,6},{9,7},{10,8},{11,9},{12,... | collective-permute-start | bytes 393224 | tf_op jit(solution)/shard_map/ppermute | solution.py:78
  43.3 7.3 %collective-permute-start.3 = (bf16[128,512]{1,0:T(8,128)(2,1)S(1)}, bf16[128,512]{1,0:T(8,128)(2,1)S(1)}, u32[]{:S(2)}, u32[]{:S(2)}) collective-permute-start(bf16[128,512]{1,0:T(8,128)(2,1)S(1)} %slice.26), channel_id=1, source_target_pairs={{0,2},{1,3},{2,4},{3,5},{4,6},{5,7},{6,8},{7,9},{8,10},{9,11},{10,... | collective-permute-start | bytes 393224 | tf_op jit(solution)/shard_map/ppermute | solution.py:78
  50.7 45.8 %collective-permute-start.8 = (bf16[8,256,512]{2,1,0:T(8,128)(2,1)S(1)}, bf16[8,256,512]{2,1,0:T(8,128)(2,1)}, u32[]{:S(2)}, u32[]{:S(2)}) collective-permute-start(bf16[8,256,512]{2,1,0:T(8,128)(2,1)S(1)} %bitcast_dynamic-update-slice_fusion), channel_id=1, source_target_pairs={{0,1},{1,0},{2,3},{3,2},{4,5},{5,4},{6,7},{7,6},{8,9},{9,8},{10,11... | collective-permute-start | bytes 6291464 | tf_op jit(solution)/shard_map/ppermute | solution.py:107
  64.8 31.7 %all-to-all-start = ((bf16[32,16,512]{2,1,0:T(8,128)(2,1)}), bf16[32,16,512]{2,1,0:T(8,128)(2,1)S(1)}, u32[]{:S(2)}, u32[]{:S(2)}) async-start(bf16[32,16,512]{2,1,0:T(8,128)(2,1)} %broadcast_select_fusion), calls=%async_computation | async-start | bytes 1048576 | tf_op jit(solution)/shard_map/all_to_all | solution.py:117
  110.7 6.5 %copy-start.3 = (bf16[8192,32]{0,1:T(8,128)(2,1)S(1)}, bf16[8192,32]{0,1:T(8,128)(2,1)}, u32[]{:S(2)}) copy-start(bf16[8192,32]{0,1:T(8,128)(2,1)} %param.13) | copy-start | bytes 1572868
  117.3 3.3 %copy-start.4 = (bf16[8192,32]{0,1:T(8,128)(2,1)S(1)}, bf16[8192,32]{0,1:T(8,128)(2,1)}, u32[]{:S(2)}) copy-start(bf16[8192,32]{0,1:T(8,128)(2,1)} %param.14) | copy-start | bytes 1572868
  117.3 21.7 %copy-start.7 = (f32[512]{0:T(512)S(1)}, f32[512]{0:T(512)}, u32[]{:S(2)}) copy-start(f32[512]{0:T(512)} %param.16) | copy-start | bytes 6148
  146.6 1.2 copy-start.1
  146.6 1.2 copy-start.2
  147.3 18.4 %copy-start.6 = (f32[512]{0:T(512)S(1)}, f32[512]{0:T(512)}, u32[]{:S(2)}) copy-start(f32[512]{0:T(512)} %param.19) | copy-start | bytes 6148
Sparse Core Ops, SparseCore 0:
  11.2 117.0 all-gather.1

commit v2 on v1

v2 whole, which is shorter than its diff:
```python
import jax
import jax.numpy as jnp
from jax import lax
from jax.experimental import pallas as pl
from jax.experimental.pallas import tpu as pltpu
from jax.sharding import PartitionSpec as P

LOG2E = 1.4426950408889634
GROUP = 8


def scan_kernel(source, half, rest, steps, maps, decay, skip, starts, out, state, squares, values, begin, landed):
    rows, width = out.shape
    copy = pltpu.make_async_copy(starts.at[source[0]], begin, landed)
    copy.start()
    projected = half[...] + rest[...].astype(jnp.float32)
    inner = projected / (1.0 + jnp.exp(-projected))
    values[...] = inner.astype(jnp.bfloat16).astype(jnp.float32)
    rate = decay[...] * -LOG2E
    size = decay.shape[0]
    gain = skip[...]
    line = lax.broadcasted_iota(jnp.int32, (GROUP, width), 0)

    def merge(low, high, bit):
        upper = (line & bit) != 0
        kept = jnp.where(upper, high, low)
        moved = jnp.where(upper, low, high)
        return kept + pltpu.roll(moved, GROUP - bit, 0)

    def advance(index, held):
        first = pl.multiple_of(index * GROUP, GROUP)
        value = values[pl.ds(first, GROUP), :]
        step = steps[pl.ds(first, GROUP), :]
        fed = step * value
        terms = []
        for at in range(GROUP):
            factor = jnp.exp2(rate * step[at : at + 1, :])
            into = jnp.tile(maps[first + at, :size], (1, width // 128))
            held = factor * held + into * fed[at : at + 1, :]
            onto = jnp.tile(maps[first + at, size:], (1, width // 128)) * held
            terms.append(onto[:GROUP] + onto[GROUP:])
        for bit in (1, 2, 4):
            terms = [merge(low, high, bit) for low, high in zip(terms[::2], terms[1::2])]
        out[pl.ds(first, GROUP), :] = terms[0] + gain * value
        return held

    copy.wait()
    state[...] = lax.fori_loop(0, rows // GROUP, advance, begin[...].astype(jnp.float32))
    whole = out[...]
    ones = jnp.ones((squares.shape[0], width), jnp.float32)
    squares[...] = lax.dot_general(
        ones,
        whole * whole,
        (((1,), (1,)), ((), ())),
        precision=lax.Precision.HIGHEST,
        preferred_element_type=jnp.float32,
    )


def run_scan(source, half, rest, steps, maps, decay, skip, starts, copies):
    rows, width = half.shape
    cells = rows * width * decay.shape[0]
    return pl.pallas_call(
        scan_kernel,
        in_specs=[pl.BlockSpec(memory_space=pltpu.SMEM)]
        + [pl.BlockSpec(memory_space=pltpu.VMEM)] * 6
        + [pl.BlockSpec(memory_space=pl.ANY)],
        scratch_shapes=[
            pltpu.VMEM((rows, width), jnp.float32),
            pltpu.VMEM(starts.shape[1:], starts.dtype),
            pltpu.SemaphoreType.DMA,
        ],
        out_shape=(
            jax.ShapeDtypeStruct((rows, width), jnp.float32),
            jax.ShapeDtypeStruct(decay.shape, jnp.float32),
            jax.ShapeDtypeStruct((copies, rows), jnp.float32),
        ),
        compiler_params=pltpu.CompilerParams(vmem_limit_bytes=32 * 1024 * 1024),
        cost_estimate=pl.CostEstimate(flops=8 * cells, bytes_accessed=8 << 20, transcendentals=cells),
    )(source, half, rest, steps, maps, decay, skip, starts)


def join_kernel(weight, more_weight, token, more_token, weights, tokens):
    for out, parts in ((weights, (weight, more_weight)), (tokens, (token, more_token))):
        rows = parts[0].shape[0]
        for at in range(2):
            out[at * rows : (at + 1) * rows, :] = parts[at][...]


def run_join(*parts):
    shapes = [jax.ShapeDtypeStruct((2 * part.shape[0], part.shape[1]), part.dtype) for part in parts[::2]]
    return pl.pallas_call(
        join_kernel,
        out_shape=tuple(shapes),
        cost_estimate=pl.CostEstimate(flops=0, bytes_accessed=2 << 20, transcendentals=0),
    )(*parts)


def token_copies(blocks, backs, whole, landed):
    rows, part = blocks[0].shape[0] // 2, blocks[0].shape[1]
    copies = []
    for slot in range(8):
        for group in range(2):
            if slot < 5:
                source = blocks[slot].at[pl.ds(group * rows, rows), :]
            else:
                source = backs[7 - slot].at[pl.ds((1 - group) * rows, rows), :]
            at = 2 * slot + group
            copies.append(
                pltpu.make_async_copy(source, whole.at[:, pl.ds(at * part, part)], landed.at[at])
            )
    return copies


def narrow_kernel(where, down, maps, *rest):
    blocks, backs = rest[:5], rest[5:8]
    kept, sent, whole, picked, landed, taken = rest[8:]
    part = blocks[0].shape[1]
    rows = kept.shape[1]
    size = maps.shape[0]
    copies = token_copies(blocks, backs, whole, landed)
    takes = []
    for at in range(16):
        for side, ref in enumerate((down, maps)):
            takes.append(
                pltpu.make_async_copy(
                    ref.at[:, pl.ds(pl.multiple_of(where[at] * part, part), part)],
                    picked.at[pl.ds(side * size, size), pl.ds(at * part, part)],
                    taken.at[len(takes)],
                )
            )
    for copy in takes + copies:
        copy.start()
    for copy in takes + copies:
        copy.wait()
    for out, first in ((kept, 0), (sent, rows)):
        out[...] = lax.dot_general(
            picked[...],
            whole[first : first + rows, :],
            (((1,), (1,)), ((), ())),
            preferred_element_type=jnp.float32,
        )


def run_narrow(where, down, maps, blocks, backs):
    rows, part = blocks[0].shape[0] // 4, blocks[0].shape[1]
    free = pl.BlockSpec(memory_space=pl.ANY)
    one = jax.ShapeDtypeStruct((2 * maps.shape[0], rows), jnp.float32)
    return pl.pallas_call(
        narrow_kernel,
        in_specs=[pl.BlockSpec(memory_space=pltpu.SMEM)] + [free] * 10,
        out_shape=(one, one),
        scratch_shapes=[
            pltpu.VMEM((2 * rows, 16 * part), jnp.bfloat16),
            pltpu.VMEM((2 * maps.shape[0], 16 * part), jnp.bfloat16),
            pltpu.SemaphoreType.DMA((16,)),
            pltpu.SemaphoreType.DMA((32,)),
        ],
        compiler_params=pltpu.CompilerParams(vmem_limit_bytes=60 * 1024 * 1024),
        cost_estimate=pl.CostEstimate(flops=1 << 28, bytes_accessed=6 << 20, transcendentals=0),
    )(where, down, maps, *blocks, *backs)


def wide_kernel(where, column, *rest):
    blocks, backs = rest[:5], rest[5:8]
    kept, sent, whole, weights, total, landed, loaded = rest[8:]
    part = blocks[0].shape[1]
    rows = kept.shape[0]
    copies = token_copies(blocks, backs, whole, landed)
    loads = [
        pltpu.make_async_copy(
            column.at[pl.ds(pl.multiple_of(where[16 + at] * part, part), part), :],
            weights.at[pl.ds(at * part, part), :],
            loaded.at[at],
        )
        for at in range(16)
    ]
    for copy, load in zip(copies, loads):
        copy.start()
        load.start()
    for first in range(0, 16, 4):
        for at in range(first, first + 4):
            copies[at].wait()
            loads[at].wait()
        span = slice(first * part, (first + 4) * part)
        added = jnp.dot(whole[:, span], weights[span, :], preferred_element_type=jnp.float32)
        if first == 0:
            total[...] = added
        elif first < 12:
            total[...] += added
        else:
            added += total[...]
            kept[...] = added[:rows]
            sent[...] = added[rows:].astype(jnp.bfloat16)


def run_wide(where, column, blocks, backs):
    rows, part = blocks[0].shape[0] // 4, blocks[0].shape[1]
    width = column.shape[1]
    free = pl.BlockSpec(memory_space=pl.ANY)
    return pl.pallas_call(
        wide_kernel,
        in_specs=[pl.BlockSpec(memory_space=pltpu.SMEM)] + [free] * 9,
        out_shape=(
            jax.ShapeDtypeStruct((rows, width), jnp.float32),
            jax.ShapeDtypeStruct((rows, width), jnp.bfloat16),
        ),
        scratch_shapes=[
            pltpu.VMEM((2 * rows, 16 * part), jnp.bfloat16),
            pltpu.VMEM((16 * part, width), jnp.bfloat16),
            pltpu.VMEM((2 * rows, width), jnp.float32),
            pltpu.SemaphoreType.DMA((16,)),
            pltpu.SemaphoreType.DMA((16,)),
        ],
        compiler_params=pltpu.CompilerParams(vmem_limit_bytes=60 * 1024 * 1024),
        cost_estimate=pl.CostEstimate(flops=1 << 31, bytes_accessed=9 << 20, transcendentals=0),
    )(where, column, *blocks, *backs)


def per_device(
    tokens,
    w_inner,
    w_bc,
    w_dt_down,
    w_dt_up,
    step_bias,
    decay_rate,
    skip_gain,
    norm_gain,
    cache,
    hits,
):
    rows, share = tokens.shape
    depth, width = w_inner.shape
    parts = lax.axis_size("tp")
    chips = parts // 2
    lines = 4
    places = lax.axis_size("req")
    planes = places // lines
    state_size = decay_rate.shape[0]
    here, place = lax.axis_index("req"), lax.axis_index("tp")
    x, y, core = here & 3, place >> 1, place & 1
    along_z = [[lines * i + j for i in range(planes)] for j in range(lines)]
    across = [(i, i ^ 2) for i in range(places)]
    beside = [(i, i ^ 1) for i in range(places)]
    swap = [(i, i ^ 1) for i in range(parts)]
    onward = [(2 * i + c, (i + 1 - 2 * c) % chips * 2 + c) for i in range(chips) for c in range(2)]

    odd = x & 1
    mine = lax.dynamic_slice_in_dim(tokens, odd * depth, depth, axis=1)
    given = lax.dynamic_slice_in_dim(tokens, (1 - odd) * depth, depth, axis=1)
    column, own = run_join(
        w_inner, lax.ppermute(w_inner, "req", across), mine, lax.ppermute(given, "req", beside)
    )

    column = lax.all_gather(column, "req", axis=0, tiled=True, axis_index_groups=along_z)

    blocks = [jnp.concatenate([own, lax.ppermute(own, "tp", swap)], axis=0)]
    for turn in range(chips // 2):
        blocks.append(lax.ppermute(blocks[-1], "tp", onward))
    backs = [lax.ppermute(block, "tp", swap) for block in blocks[1:4]]

    at = jnp.arange(2 * chips, dtype=jnp.int32)
    chip = (y - (1 - 2 * core) * (at >> 1)) & 7
    side = core ^ (at & 1)
    where = jnp.concatenate([lines * chip + 2 * side + odd, 2 * chip + (side ^ (x >> 1))])

    states = jnp.take(cache[0].astype(jnp.bfloat16), hits[:, 1] - 1, axis=0, mode="clip")
    states = lax.all_to_all(states, "req", split_axis=0, concat_axis=0, tiled=True)
    source = lax.dynamic_slice_in_dim(hits[:, 0], here, 1)

    kept, sent = run_narrow(where, w_dt_down.T, w_bc.T, blocks, backs)
    narrow = kept + lax.ppermute(sent, "req", beside)
    half, sent = run_wide(where, column, blocks, backs)
    rest = lax.ppermute(sent, "req", beside)

    low = lax.all_gather(narrow[:32].astype(jnp.bfloat16), "tp", axis=0, tiled=True)
    spread = jnp.broadcast_to(jnp.transpose(narrow[32:])[:, :, None], (rows, 2 * state_size, 128))
    step = jax.nn.softplus(
        lax.dot_general(low, w_dt_up, (((0,), (0,)), ((), ())), preferred_element_type=jnp.float32)
        + step_bias[None, :]
    )
    out, state, squares = run_scan(
        source, half, rest, step, spread, decay_rate, skip_gain[None, :], states, parts
    )
    sums = jnp.sum(lax.all_to_all(squares, "tp", split_axis=0, concat_axis=0, tiled=True), axis=0)
    scale = lax.rsqrt(sums / (width * parts) + 1e-05)
    normed = (out * scale[:, None] * norm_gain[None, :]).astype(jnp.bfloat16)
    return (normed, state.reshape(1, state_size, width))


def solution(mesh):
    placed = (
        P("req", "tp"),
        P("req", "tp"),
        P(),
        P(None, "tp"),
        P(None, "tp"),
        P("tp"),
        P(None, "tp"),
        P("tp"),
        P("tp"),
        P("req", None, None, "tp"),
        P(),
    )
    return jax.shard_map(
        per_device,
        mesh=mesh,
        in_specs=placed,
        out_specs=(P("req", "tp"), P("req", None, "tp")),
        check_vma=False,
    )
```

time: 174 us -> 156 us (0.90)
  Pallas kernels: 3.81 us -> 17.9 us
  waiting for transfers between devices: 34 us -> 20.6 us
  matrix products: 13.8 us -> 0.55 us
  local copies, waits for them, and re-layouts: 15.3 us -> 6.65 us
  starting transfers between devices: 49.7 us -> 57.3 us
  other arithmetic: 11.2 us -> 4.15 us
  blocking collectives: 29.2 us -> 34.1 us
  between operations: 16.4 us -> 14.4 us
    all_to_all x1, waiting for transfers between devices: 20.7 us -> 0.01 us  [per_device(): lax.all_to_all(states, 'req', split_axis=0, concat_axis=0, tiled=True)]
    pallas_call x1 -> x4, Pallas kernels: 3.81 us -> 17.9 us  [the longest x1 5.83 us: run_wide(): pl.pallas_call(wide_kernel, in_specs=[pl.BlockSpec(memory_space=pltpu.SME...]
    dot_general x4 -> x1, matrix products: 13.8 us -> 0.55 us  [per_device(): lax.dot_general(low, w_dt_up, (((0,), (0,)), ((), ())), preferred_element...]
    select_n x5 -> x0, other arithmetic: 10.2 us -> none  [the longest x2 4.7 us: per_device(): jnp.take(pair, order, axis=0)]
    ppermute x9 -> x12, waiting for transfers between devices: 12.6 us -> 20.6 us  [the longest x4 13.5 us: per_device(): blocks.append(lax.ppermute(blocks[-1], 'tp', onward))]
    select_n x1 -> x0, local copies, waits for them, and re-layouts: 6.51 us -> none  [per_device(): jnp.take(pair, order, axis=0)]
    all_gather x1, blocking collectives: 15.3 us -> 20.7 us  [per_device(): lax.all_gather(narrow[:32].astype(jnp.bfloat16), 'tp', axis=0, tiled=True)]
    ppermute x9 -> x12, starting transfers between devices: 41.3 us -> 46.1 us  [the longest x4 19.4 us: per_device(): blocks.append(lax.ppermute(blocks[-1], 'tp', onward))]
  transfers between devices with their start and end apart: 11 -> 14, of which waited for: 6 -> 6; matrix products, arithmetic and copies ran while one was open for 18% -> 5% of each run, Pallas kernels for 0% -> 7%
where the time goes in v2:
time: 156 us
  starting transfers between devices  57.3 us (37%)
  blocking collectives  34.1 us (22%)
  waiting for transfers between devices  20.6 us (13%)
  Pallas kernels  17.9 us (11%)
  between operations  14.4 us (9%)
  local copies, waits for them, and re-layouts  6.65 us (4%)
  other arithmetic  4.15 us (3%)
    all_gather x1, blocking collectives, per_device(): lax.all_gather(narrow[:32].astype(jnp.bfloat16), 'tp', axis=0, tiled=True)  20.7 us
    ppermute x4, starting transfers between devices, per_device(): blocks.append(lax.ppermute(blocks[-1], 'tp', onward))  19.4 us
    ppermute x4, waiting for transfers between devices, per_device(): blocks.append(lax.ppermute(blocks[-1], 'tp', onward))  13.5 us
    all_to_all x1, blocking collectives, per_device(): lax.all_to_all(squares, 'tp', split_axis=0, concat_axis=0, tiled=True)  13.4 us
    all_to_all x1, starting transfers between devices, per_device(): lax.all_to_all(states, 'req', split_axis=0, concat_axis=0, tiled=True)  11.2 us
    ppermute x3, starting transfers between devices, per_device(): backs = [lax.ppermute(block, 'tp', swap) for block in blocks[1:4]]  7.33 us
    pallas_call x1, Pallas kernels, run_wide(): pl.pallas_call(wide_kernel, in_specs=[pl.BlockSpec(memory_space=pltpu.SME...  5.83 us
    ppermute x1, starting transfers between devices, per_device(): lax.ppermute(w_inner, 'req', across)  5.62 us
  transfers between devices with their start and end apart: 14, of which 6 were waited for; matrix products, arithmetic and copies ran while one was open for 5% of the time, Pallas kernels for 7%

profile of v2, /device:TPU:1, one launch (start us, length us, event | category | flops | bytes accessed | tf_op | source)
XLA Modules:
  0.0 155.7 jit_solution(12883707673275460420)
XLA Ops:
  7.2 5.6 %collective-permute-start = (bf16[256,512]{1,0:T(8,128)(2,1)}, bf16[256,512]{1,0:T(8,128)(2,1)S(1)}, u32[]{:S(2)}, u32[]{:S(2)}) collective-permute-start(bf16[256,512]{1,0:T(8,128)(2,1)} %weight.1), channel_id=1, source_target_pairs={{0,32},{16,48},{32,0},{48,16},{64,96},{80,112},{96,64},{112,80},{1... | collective-permute-start | bytes 786440 | tf_op jit(solution)/shard_map/ppermute | solution.py:253
  12.9 1.6 %constant_dynamic-slice_fusion = (bf16[256,256]{1,0:T(8,128)(2,1)S(1)}, bf16[256,256]{1,0:T(8,128)(2,1)}) fusion(bf16[256,512]{1,0:T(8,128)(2,1)} %param.11, s32[]{:T(128)S(6)} %select_n.15, s32[]{:T(128)S(6)} %select_n.14), kind=kLoop, calls=%fused_computation.11 | loop fusion | bytes 524296 | tf_op jit(solution)/shard_map/dynamic_slice | solution.py:251
  14.5 2.2 %collective-permute-start.1 = (bf16[256,256]{1,0:T(8,128)(2,1)S(1)}, bf16[256,256]{1,0:T(8,128)(2,1)S(1)}, u32[]{:S(2)}, u32[]{:S(2)}) collective-permute-start(bf16[256,256]{1,0:T(8,128)(2,1)S(1)} %get-tuple-element.20), channel_id=1, source_target_pairs={{0,16},{16,0},{32,48},{48,32},{64,80},{80,64},{96,112},{112,96},{1... | collective-permute-start | bytes 393224 | tf_op jit(solution)/shard_map/ppermute | solution.py:253
  16.7 4.9 %collective-permute-done.1.more_token = bf16[256,256]{1,0:T(8,128)(2,1)S(1)} collective-permute-done((bf16[256,256]{1,0:T(8,128)(2,1)S(1)}, bf16[256,256]{1,0:T(8,128)(2,1)S(1)}, u32[]{:S(2)}, u32[]{:S(2)}) %collective-permute-start.1) | collective-permute-done | bytes 131104 | tf_op jit(solution)/shard_map/ppermute | solution.py:253
  22.4 2.0 %shard_map.122 = (bf16[512,512]{1,0:T(8,128)(2,1)}, bf16[512,256]{1,0:T(8,128)(2,1)}) custom-call(bf16[256,512]{1,0:T(8,128)(2,1)} %weight.1, bf16[256,512]{1,0:T(8,128)(2,1)} %copy-done.8, bf16[256,256]{1,0:T(8,128)(2,1)} %get-tuple-element.21.token, bf16[256,256]{1,0:T(8,128)(2,1)} %copy-done.9), custom_call_target="tpu_custom_call" | custom-call | bytes 2097152 | tf_op jit(solution)/shard_map/pallas_call | solution.py:92
  24.4 5.0 %collective-permute-start.2 = (bf16[512,256]{1,0:T(8,128)(2,1)}, bf16[512,256]{1,0:T(8,128)(2,1)S(1)}, u32[]{:S(2)}, u32[]{:S(2)}) collective-permute-start(bf16[512,256]{1,0:T(8,128)(2,1)} %get-tuple-element.12), channel_id=1, source_target_pairs={{0,1},{1,0},{2,3},{3,2},{4,5},{5,4},{6,7},{7,6},{8,9},{9,8},{10,11... | collective-permute-start | bytes 786440 | tf_op jit(solution)/shard_map/ppermute | solution.py:258
  30.8 3.8 %collective-permute-start.3 = (bf16[1024,256]{1,0:T(8,128)(2,1)S(1)}, bf16[1024,256]{1,0:T(8,128)(2,1)S(1)}, u32[]{:S(2)}, u32[]{:S(2)}) collective-permute-start(bf16[1024,256]{1,0:T(8,128)(2,1)S(1)} %constant_dynamic-update-slice_fusion.rest_0_), channel_id=1, source_target_pairs={{0,2},{1,15},{2,4},{3,1},{4,6},{5,3},{6,8},{7,5},{8,10},{9,7},{10,... | collective-permute-start | bytes 1572872 | tf_op jit(solution)/shard_map/ppermute | solution.py:260
  34.6 6.4 %collective-permute-done.3.rest_1_ = bf16[1024,256]{1,0:T(8,128)(2,1)S(1)} collective-permute-done((bf16[1024,256]{1,0:T(8,128)(2,1)S(1)}, bf16[1024,256]{1,0:T(8,128)(2,1)S(1)}, u32[]{:S(2)}, u32[]{:S(2)}) %collective-permute-start.3) | collective-permute-done | bytes 524320 | tf_op jit(solution)/shard_map/ppermute | solution.py:260
  41.0 4.7 %collective-permute-start.4 = (bf16[1024,256]{1,0:T(8,128)(2,1)S(1)}, bf16[1024,256]{1,0:T(8,128)(2,1)S(1)}, u32[]{:S(2)}, u32[]{:S(2)}) collective-permute-start(bf16[1024,256]{1,0:T(8,128)(2,1)S(1)} %collective-permute-done.3.rest_1_), channel_id=1, source_target_pairs={{0,2},{1,15},{2,4},{3,1},{4,6},{5,3},{6,8},{7,5},{8,10},{9,7},{10,... | collective-permute-start | bytes 1572872 | tf_op jit(solution)/shard_map/ppermute | solution.py:260
  45.7 6.1 %collective-permute-done.4.rest_2_ = bf16[1024,256]{1,0:T(8,128)(2,1)S(1)} collective-permute-done((bf16[1024,256]{1,0:T(8,128)(2,1)S(1)}, bf16[1024,256]{1,0:T(8,128)(2,1)S(1)}, u32[]{:S(2)}, u32[]{:S(2)}) %collective-permute-start.4) | collective-permute-done | bytes 524320 | tf_op jit(solution)/shard_map/ppermute | solution.py:260
  51.8 5.4 %collective-permute-start.5 = (bf16[1024,256]{1,0:T(8,128)(2,1)S(1)}, bf16[1024,256]{1,0:T(8,128)(2,1)S(1)}, u32[]{:S(2)}, u32[]{:S(2)}) collective-permute-start(bf16[1024,256]{1,0:T(8,128)(2,1)S(1)} %collective-permute-done.4.rest_2_), channel_id=1, source_target_pairs={{0,2},{1,15},{2,4},{3,1},{4,6},{5,3},{6,8},{7,5},{8,10},{9,7},{10,... | collective-permute-start | bytes 1572872 | tf_op jit(solution)/shard_map/ppermute | solution.py:260
  58.0 2.2 %collective-permute-start.7 = (bf16[1024,256]{1,0:T(8,128)(2,1)S(1)}, bf16[1024,256]{1,0:T(8,128)(2,1)}, u32[]{:S(2)}, u32[]{:S(2)}) collective-permute-start(bf16[1024,256]{1,0:T(8,128)(2,1)S(1)} %collective-permute-done.3.rest_1_), channel_id=1, source_target_pairs={{0,1},{1,0},{2,3},{3,2},{4,5},{5,4},{6,7},{7,6},{8,9},{9,8},{10,11... | collective-permute-start | bytes 1572872 | tf_op jit(solution)/shard_map/ppermute | solution.py:261
  60.3 2.1 %collective-permute-start.8 = (bf16[1024,256]{1,0:T(8,128)(2,1)S(1)}, bf16[1024,256]{1,0:T(8,128)(2,1)}, u32[]{:S(2)}, u32[]{:S(2)}) collective-permute-start(bf16[1024,256]{1,0:T(8,128)(2,1)S(1)} %collective-permute-done.4.rest_2_), channel_id=1, source_target_pairs={{0,1},{1,0},{2,3},{3,2},{4,5},{5,4},{6,7},{7,6},{8,9},{9,8},{10,11... | collective-permute-start | bytes 1572872 | tf_op jit(solution)/shard_map/ppermute | solution.py:261
  63.4 5.4 %collective-permute-start.6 = (bf16[1024,256]{1,0:T(8,128)(2,1)S(1)}, bf16[1024,256]{1,0:T(8,128)(2,1)}, u32[]{:S(2)}, u32[]{:S(2)}) collective-permute-start(bf16[1024,256]{1,0:T(8,128)(2,1)S(1)} %collective-permute-done.5.rest_3_), channel_id=1, source_target_pairs={{0,2},{1,15},{2,4},{3,1},{4,6},{5,3},{6,8},{7,5},{8,10},{9,7},{10,... | collective-permute-start | bytes 1572872 | tf_op jit(solution)/shard_map/ppermute | solution.py:260
  68.8 3.0 %collective-permute-start.9 = (bf16[1024,256]{1,0:T(8,128)(2,1)S(1)}, bf16[1024,256]{1,0:T(8,128)(2,1)}, u32[]{:S(2)}, u32[]{:S(2)}) collective-permute-start(bf16[1024,256]{1,0:T(8,128)(2,1)S(1)} %collective-permute-done.5.rest_3_), channel_id=1, source_target_pairs={{0,1},{1,0},{2,3},{3,2},{4,5},{5,4},{6,7},{7,6},{8,9},{9,8},{10,11... | collective-permute-start | bytes 1572872 | tf_op jit(solution)/shard_map/ppermute | solution.py:261
  74.3 11.2 %all-to-all-start = ((bf16[32,16,512]{2,1,0:T(8,128)(2,1)}), bf16[32,16,512]{2,1,0:T(8,128)(2,1)S(1)}, u32[]{:S(2)}, u32[]{:S(2)}) async-start(bf16[32,16,512]{2,1,0:T(8,128)(2,1)} %gather_fusion), calls=%async_computation | async-start | bytes 1048576 | tf_op jit(solution)/shard_map/all_to_all | solution.py:269
  86.2 5.5 %shard_map.124 = (f32[64,256]{1,0:T(8,128)}, f32[64,256]{1,0:T(8,128)}) custom-call(s32[32]{0:T(128)} %pad_add_fusion.where, bf16[32,8192]{1,0:T(8,128)(2,1)} %bitcast.16, bf16[32,8192]{1,0:T(8,128)(2,1)} %bitcast.17, bf16[1024,256]{1,0:T(8,128)(2,1)} %copy-done.4, bf16[1024,256]{1,0:T(8,128)(2,1)} %copy-done.5, bf16[1024,256]{1,0:T(8,128)(2,1)} %copy-done.6, ...), custom_call_target="tpu_custom_call" | custom-call | flops 268435456 | bytes 6291456 | tf_op jit(solution)/shard_map/pallas_call | solution.py:149
  91.7 3.1 %collective-permute-start.11 = (f32[64,256]{1,0:T(8,128)}, f32[64,256]{1,0:T(8,128)S(1)}, u32[]{:S(2)}, u32[]{:S(2)}) collective-permute-start(f32[64,256]{1,0:T(8,128)} %get-tuple-element.16), channel_id=1, source_target_pairs={{0,16},{16,0},{32,48},{48,32},{64,80},{80,64},{96,112},{112,96},{1... | collective-permute-start | bytes 196616 | tf_op jit(solution)/shard_map/ppermute | solution.py:273
  95.4 1.8 %collective-permute-done.11 = f32[64,256]{1,0:T(8,128)S(1)} collective-permute-done((f32[64,256]{1,0:T(8,128)}, f32[64,256]{1,0:T(8,128)S(1)}, u32[]{:S(2)}, u32[]{:S(2)}) %collective-permute-start.11) | collective-permute-done | bytes 65568 | tf_op jit(solution)/shard_map/ppermute | solution.py:273
  98.1 5.8 %shard_map.123 = (f32[256,512]{1,0:T(8,128)}, bf16[256,512]{1,0:T(8,128)(2,1)}) custom-call(s32[32]{0:T(128)} %pad_add_fusion.where, bf16[4096,512]{1,0:T(8,128)(2,1)} %all-gather.2.cloned.1.call-done.column, bf16[1024,256]{1,0:T(8,128)(2,1)} %copy-done.4, bf16[1024,256]{1,0:T(8,128)(2,1)} %copy-done.5, bf16[1024,256]{1,0:T(8,128)(2,1)} %copy-done.6, ...), custom_call_target="tpu_custom_call" | custom-call | flops 2147483648 | bytes 9437184 | tf_op jit(solution)/shard_map/pallas_call | solution.py:201
  104.0 3.4 %collective-permute-start.10 = (bf16[256,512]{1,0:T(8,128)(2,1)}, bf16[256,512]{1,0:T(8,128)(2,1)S(1)}, u32[]{:S(2)}, u32[]{:S(2)}) collective-permute-start(bf16[256,512]{1,0:T(8,128)(2,1)} %get-tuple-element.14), channel_id=1, source_target_pairs={{0,16},{16,0},{32,48},{48,32},{64,80},{80,64},{96,112},{112,96},{1... | collective-permute-start | bytes 786440 | tf_op jit(solution)/shard_map/ppermute | solution.py:275
  107.4 20.7 %all_gather.7 = bf16[512,256]{1,0:T(8,128)(2,1)S(1)} all-gather(bf16[32,256]{1,0:T(8,128)(2,1)S(1)} %slice.24), channel_id=1, replica_groups=mesh['req'=32,'tp'=16] {'tp'}, dimensions={0}, use_global_device_ids=true | all-gather | bytes 278528 | tf_op jit(solution)/shard_map/all_gather | solution.py:277
  130.0 4.5 %shard_map.125 = (f32[256,512]{1,0:T(8,128)S(1)}, f32[16,512]{1,0:T(8,128)}, f32[16,256]{1,0:T(8,128)S(1)}) custom-call(s32[1]{0:T(128)} %bitcast.source, f32[256,512]{1,0:T(8,128)S(1)} %copy-done.1, bf16[256,512]{1,0:T(8,128)(2,1)S(1)} %collective-permute-done.10.rest, f32[256,512]{1,0:T(8,128)S(1)} %compare_select_fusion.steps, ...), custom_call_target="tpu_custom_call" | custom-call | flops 16777216 | bytes 8388608 | tf_op jit(solution)/shard_map/pallas_call | solution.py:63
  134.6 13.4 %all_to_all.14 = f32[16,1,256]{2,1,0:T(1,128)S(1)} all-to-all(f32[16,1,256]{2,1,0:T(1,128)S(1)} %copy.15), channel_id=1, replica_groups=mesh['req'=32,'tp'=16] {'tp'}, dimensions={0} | all-to-all | bytes 32768 | tf_op jit(solution)/shard_map/all_to_all | solution.py:286
  (55 shorter events, 11.2 us)
Async XLA Ops:
  7.2 121.1 %copy-start = (bf16[512,512]{1,0:T(8,128)(2,1)S(1)}, bf16[512,512]{1,0:T(8,128)(2,1)}, u32[]{:S(2)}) copy-start(bf16[512,512]{1,0:T(8,128)(2,1)} %param.15) | copy-start | bytes 1572868
  7.2 90.9 %all-gather.2.cloned.1.call-start = ((), (), s32[]{:S(2)}) async-start(), calls=%async_computation.2 | async-start | bytes 4718592 | tf_op jit(solution)/shard_map/all_gather | solution.py:256
  7.2 14.4 %collective-permute-start = (bf16[256,512]{1,0:T(8,128)(2,1)}, bf16[256,512]{1,0:T(8,128)(2,1)S(1)}, u32[]{:S(2)}, u32[]{:S(2)}) collective-permute-start(bf16[256,512]{1,0:T(8,128)(2,1)} %weight.1), channel_id=1, source_target_pairs={{0,32},{16,48},{32,0},{48,16},{64,96},{80,112},{96,64},{112,80},{1... | collective-permute-start | bytes 786440 | tf_op jit(solution)/shard_map/ppermute | solution.py:253
  14.5 7.1 %collective-permute-start.1 = (bf16[256,256]{1,0:T(8,128)(2,1)S(1)}, bf16[256,256]{1,0:T(8,128)(2,1)S(1)}, u32[]{:S(2)}, u32[]{:S(2)}) collective-permute-start(bf16[256,256]{1,0:T(8,128)(2,1)S(1)} %get-tuple-element.20), channel_id=1, source_target_pairs={{0,16},{16,0},{32,48},{48,32},{64,80},{80,64},{96,112},{112,96},{1... | collective-permute-start | bytes 393224 | tf_op jit(solution)/shard_map/ppermute | solution.py:253
  24.4 6.3 %collective-permute-start.2 = (bf16[512,256]{1,0:T(8,128)(2,1)}, bf16[512,256]{1,0:T(8,128)(2,1)S(1)}, u32[]{:S(2)}, u32[]{:S(2)}) collective-permute-start(bf16[512,256]{1,0:T(8,128)(2,1)} %get-tuple-element.12), channel_id=1, source_target_pairs={{0,1},{1,0},{2,3},{3,2},{4,5},{5,4},{6,7},{7,6},{8,9},{9,8},{10,11... | collective-permute-start | bytes 786440 | tf_op jit(solution)/shard_map/ppermute | solution.py:258
  30.8 55.4 %copy-start.4 = (bf16[1024,256]{1,0:T(8,128)(2,1)}, bf16[1024,256]{1,0:T(8,128)(2,1)S(1)}, u32[]{:S(2)}) copy-start(bf16[1024,256]{1,0:T(8,128)(2,1)S(1)} %constant_dynamic-update-slice_fusion.rest_0_) | copy-start | bytes 1572868
  30.8 10.2 %collective-permute-start.3 = (bf16[1024,256]{1,0:T(8,128)(2,1)S(1)}, bf16[1024,256]{1,0:T(8,128)(2,1)S(1)}, u32[]{:S(2)}, u32[]{:S(2)}) collective-permute-start(bf16[1024,256]{1,0:T(8,128)(2,1)S(1)} %constant_dynamic-update-slice_fusion.rest_0_), channel_id=1, source_target_pairs={{0,2},{1,15},{2,4},{3,1},{4,6},{5,3},{6,8},{7,5},{8,10},{9,7},{10,... | collective-permute-start | bytes 1572872 | tf_op jit(solution)/shard_map/ppermute | solution.py:260
  41.0 45.1 %copy-start.5 = (bf16[1024,256]{1,0:T(8,128)(2,1)}, bf16[1024,256]{1,0:T(8,128)(2,1)S(1)}, u32[]{:S(2)}) copy-start(bf16[1024,256]{1,0:T(8,128)(2,1)S(1)} %collective-permute-done.3.rest_1_) | copy-start | bytes 1572868
  41.0 10.9 %collective-permute-start.4 = (bf16[1024,256]{1,0:T(8,128)(2,1)S(1)}, bf16[1024,256]{1,0:T(8,128)(2,1)S(1)}, u32[]{:S(2)}, u32[]{:S(2)}) collective-permute-start(bf16[1024,256]{1,0:T(8,128)(2,1)S(1)} %collective-permute-done.3.rest_1_), channel_id=1, source_target_pairs={{0,2},{1,15},{2,4},{3,1},{4,6},{5,3},{6,8},{7,5},{8,10},{9,7},{10,... | collective-permute-start | bytes 1572872 | tf_op jit(solution)/shard_map/ppermute | solution.py:260
  51.8 34.3 %copy-start.6 = (bf16[1024,256]{1,0:T(8,128)(2,1)}, bf16[1024,256]{1,0:T(8,128)(2,1)S(1)}, u32[]{:S(2)}) copy-start(bf16[1024,256]{1,0:T(8,128)(2,1)S(1)} %collective-permute-done.4.rest_2_) | copy-start | bytes 1572868
  51.8 11.5 %collective-permute-start.5 = (bf16[1024,256]{1,0:T(8,128)(2,1)S(1)}, bf16[1024,256]{1,0:T(8,128)(2,1)S(1)}, u32[]{:S(2)}, u32[]{:S(2)}) collective-permute-start(bf16[1024,256]{1,0:T(8,128)(2,1)S(1)} %collective-permute-done.4.rest_2_), channel_id=1, source_target_pairs={{0,2},{1,15},{2,4},{3,1},{4,6},{5,3},{6,8},{7,5},{8,10},{9,7},{10,... | collective-permute-start | bytes 1572872 | tf_op jit(solution)/shard_map/ppermute | solution.py:260
  58.0 28.1 %collective-permute-start.7 = (bf16[1024,256]{1,0:T(8,128)(2,1)S(1)}, bf16[1024,256]{1,0:T(8,128)(2,1)}, u32[]{:S(2)}, u32[]{:S(2)}) collective-permute-start(bf16[1024,256]{1,0:T(8,128)(2,1)S(1)} %collective-permute-done.3.rest_1_), channel_id=1, source_target_pairs={{0,1},{1,0},{2,3},{3,2},{4,5},{5,4},{6,7},{7,6},{8,9},{9,8},{10,11... | collective-permute-start | bytes 1572872 | tf_op jit(solution)/shard_map/ppermute | solution.py:261
  60.3 25.8 %collective-permute-start.8 = (bf16[1024,256]{1,0:T(8,128)(2,1)S(1)}, bf16[1024,256]{1,0:T(8,128)(2,1)}, u32[]{:S(2)}, u32[]{:S(2)}) collective-permute-start(bf16[1024,256]{1,0:T(8,128)(2,1)S(1)} %collective-permute-done.4.rest_2_), channel_id=1, source_target_pairs={{0,1},{1,0},{2,3},{3,2},{4,5},{5,4},{6,7},{7,6},{8,9},{9,8},{10,11... | collective-permute-start | bytes 1572872 | tf_op jit(solution)/shard_map/ppermute | solution.py:261
  63.4 22.8 %copy-start.7 = (bf16[1024,256]{1,0:T(8,128)(2,1)}, bf16[1024,256]{1,0:T(8,128)(2,1)S(1)}, u32[]{:S(2)}) copy-start(bf16[1024,256]{1,0:T(8,128)(2,1)S(1)} %collective-permute-done.5.rest_3_) | copy-start | bytes 1572868
  63.4 22.7 %collective-permute-start.6 = (bf16[1024,256]{1,0:T(8,128)(2,1)S(1)}, bf16[1024,256]{1,0:T(8,128)(2,1)}, u32[]{:S(2)}, u32[]{:S(2)}) collective-permute-start(bf16[1024,256]{1,0:T(8,128)(2,1)S(1)} %collective-permute-done.5.rest_3_), channel_id=1, source_target_pairs={{0,2},{1,15},{2,4},{3,1},{4,6},{5,3},{6,8},{7,5},{8,10},{9,7},{10,... | collective-permute-start | bytes 1572872 | tf_op jit(solution)/shard_map/ppermute | solution.py:260
  68.8 17.3 %collective-permute-start.9 = (bf16[1024,256]{1,0:T(8,128)(2,1)S(1)}, bf16[1024,256]{1,0:T(8,128)(2,1)}, u32[]{:S(2)}, u32[]{:S(2)}) collective-permute-start(bf16[1024,256]{1,0:T(8,128)(2,1)S(1)} %collective-permute-done.5.rest_3_), channel_id=1, source_target_pairs={{0,1},{1,0},{2,3},{3,2},{4,5},{5,4},{6,7},{7,6},{8,9},{9,8},{10,11... | collective-permute-start | bytes 1572872 | tf_op jit(solution)/shard_map/ppermute | solution.py:261
  74.3 54.5 %all-to-all-start = ((bf16[32,16,512]{2,1,0:T(8,128)(2,1)}), bf16[32,16,512]{2,1,0:T(8,128)(2,1)S(1)}, u32[]{:S(2)}, u32[]{:S(2)}) async-start(bf16[32,16,512]{2,1,0:T(8,128)(2,1)} %gather_fusion), calls=%async_computation | async-start | bytes 1048576 | tf_op jit(solution)/shard_map/all_to_all | solution.py:269
  91.7 5.5 %collective-permute-start.11 = (f32[64,256]{1,0:T(8,128)}, f32[64,256]{1,0:T(8,128)S(1)}, u32[]{:S(2)}, u32[]{:S(2)}) collective-permute-start(f32[64,256]{1,0:T(8,128)} %get-tuple-element.16), channel_id=1, source_target_pairs={{0,16},{16,0},{32,48},{48,32},{64,80},{80,64},{96,112},{112,96},{1... | collective-permute-start | bytes 196616 | tf_op jit(solution)/shard_map/ppermute | solution.py:273
  98.1 30.2 %copy-start.11 = (f32[512]{0:T(512)S(1)}, f32[512]{0:T(512)}, u32[]{:S(2)}) copy-start(f32[512]{0:T(512)} %param.16) | copy-start | bytes 6148
  104.0 26.0 %copy-start.1 = (f32[256,512]{1,0:T(8,128)S(1)}, f32[256,512]{1,0:T(8,128)}, u32[]{:S(2)}) copy-start(f32[256,512]{1,0:T(8,128)} %get-tuple-element.13.half) | copy-start | bytes 1572868
  104.0 26.0 %copy-start.2 = (f32[16,512]{1,0:T(8,128)S(1)}, f32[16,512]{1,0:T(8,128)}, u32[]{:S(2)}) copy-start(f32[16,512]{1,0:T(8,128)} %decay.1) | copy-start | bytes 98308
  104.0 26.0 %copy-start.3 = (f32[512]{0:T(512)S(1)}, f32[512]{0:T(512)}, u32[]{:S(2)}) copy-start(f32[512]{0:T(512)} %param.18) | copy-start | bytes 6148
  104.0 24.8 %collective-permute-start.10 = (bf16[256,512]{1,0:T(8,128)(2,1)}, bf16[256,512]{1,0:T(8,128)(2,1)S(1)}, u32[]{:S(2)}, u32[]{:S(2)}) collective-permute-start(bf16[256,512]{1,0:T(8,128)(2,1)} %get-tuple-element.14), channel_id=1, source_target_pairs={{0,16},{16,0},{32,48},{48,32},{64,80},{80,64},{96,112},{112,96},{1... | collective-permute-start | bytes 786440 | tf_op jit(solution)/shard_map/ppermute | solution.py:275
  128.8 19.2 %copy-start.10 = (f32[512]{0:T(512)S(1)}, f32[512]{0:T(512)}, u32[]{:S(2)}) copy-start(f32[512]{0:T(512)} %param.19) | copy-start | bytes 6148
  (2 other events, 1.4 us)
Sparse Core Ops, SparseCore 0:
  24.5 63.0 all-gather.1

commit v3 on v2

--- a/solution.py
+++ b/solution.py
@@ -46,15 +46,16 @@
 
     copy.wait()
     state[...] = lax.fori_loop(0, rows // GROUP, advance, begin[...].astype(jnp.float32))
-    whole = out[...]
-    ones = jnp.ones((squares.shape[0], width), jnp.float32)
-    squares[...] = lax.dot_general(
-        ones,
-        whole * whole,
-        (((1,), (1,)), ((), ())),
-        precision=lax.Precision.HIGHEST,
-        preferred_element_type=jnp.float32,
-    )
+    square = out[...] * out[...]
+    ones = jnp.ones((squares.shape[0], width), jnp.bfloat16)
+    total = jnp.zeros(squares.shape, jnp.float32)
+    for _ in range(3):
+        high = square.astype(jnp.bfloat16)
+        square -= high.astype(jnp.float32)
+        total += lax.dot_general(
+            ones, high, (((1,), (1,)), ((), ())), preferred_element_type=jnp.float32
+        )
+    squares[...] = total
 
 
 def run_scan(source, half, rest, steps, maps, decay, skip, starts, copies):
@@ -112,61 +113,14 @@
     return copies
 
 
-def narrow_kernel(where, down, maps, *rest):
-    blocks, backs = rest[:5], rest[5:8]
-    kept, sent, whole, picked, landed, taken = rest[8:]
+def project_kernel(where, down, maps, *rest):
+    blocks, backs, column = rest[:5], rest[5:8], rest[8]
+    narrow, narrow_sent, kept, sent, whole, thin, picked, weights, landed, taken, loaded = rest[9:]
     part = blocks[0].shape[1]
-    rows = kept.shape[1]
+    rows = kept.shape[0]
     size = maps.shape[0]
     copies = token_copies(blocks, backs, whole, landed)
-    takes = []
-    for at in range(16):
-        for side, ref in enumerate((down, maps)):
-            takes.append(
-                pltpu.make_async_copy(
-                    ref.at[:, pl.ds(pl.multiple_of(where[at] * part, part), part)],
-                    picked.at[pl.ds(side * size, size), pl.ds(at * part, part)],
-                    taken.at[len(takes)],
-                )
-            )
-    for copy in takes + copies:
-        copy.start()
-    for copy in takes + copies:
-        copy.wait()
-    for out, first in ((kept, 0), (sent, rows)):
-        out[...] = lax.dot_general(
-            picked[...],
-            whole[first : first + rows, :],
-            (((1,), (1,)), ((), ())),
-            preferred_element_type=jnp.float32,
-        )
-
-
-def run_narrow(where, down, maps, blocks, backs):
-    rows, part = blocks[0].shape[0] // 4, blocks[0].shape[1]
-    free = pl.BlockSpec(memory_space=pl.ANY)
-    one = jax.ShapeDtypeStruct((2 * maps.shape[0], rows), jnp.float32)
-    return pl.pallas_call(
-        narrow_kernel,
-        in_specs=[pl.BlockSpec(memory_space=pltpu.SMEM)] + [free] * 10,
-        out_shape=(one, one),
-        scratch_shapes=[
-            pltpu.VMEM((2 * rows, 16 * part), jnp.bfloat16),
-            pltpu.VMEM((2 * maps.shape[0], 16 * part), jnp.bfloat16),
-            pltpu.SemaphoreType.DMA((16,)),
-            pltpu.SemaphoreType.DMA((32,)),
-        ],
-        compiler_params=pltpu.CompilerParams(vmem_limit_bytes=60 * 1024 * 1024),
-        cost_estimate=pl.CostEstimate(flops=1 << 28, bytes_accessed=6 << 20, transcendentals=0),
-    )(where, down, maps, *blocks, *backs)
-
-
-def wide_kernel(where, column, *rest):
-    blocks, backs = rest[:5], rest[5:8]
-    kept, sent, whole, weights, total, landed, loaded = rest[8:]
-    part = blocks[0].shape[1]
-    rows = kept.shape[0]
-    copies = token_copies(blocks, backs, whole, landed)
+    takes = [pltpu.make_async_copy(ref, thin.at[at], taken.at[at]) for at, ref in enumerate((down, maps))]
     loads = [
         pltpu.make_async_copy(
             column.at[pl.ds(pl.multiple_of(where[16 + at] * part, part), part), :],
@@ -175,46 +129,59 @@
         )
         for at in range(16)
     ]
-    for copy, load in zip(copies, loads):
+    for copy in takes + copies + loads:
         copy.start()
-        load.start()
-    for first in range(0, 16, 4):
-        for at in range(first, first + 4):
-            copies[at].wait()
-            loads[at].wait()
-        span = slice(first * part, (first + 4) * part)
-        added = jnp.dot(whole[:, span], weights[span, :], preferred_element_type=jnp.float32)
-        if first == 0:
-            total[...] = added
-        elif first < 12:
-            total[...] += added
-        else:
-            added += total[...]
-            kept[...] = added[:rows]
-            sent[...] = added[rows:].astype(jnp.bfloat16)
-
-
-def run_wide(where, column, blocks, backs):
+    for take in takes:
+        take.wait()
+    for at in range(16):
+        first = pl.multiple_of(where[at] * part, part)
+        for side in range(2):
+            picked[side * size : (side + 1) * size, at * part : (at + 1) * part] = thin[
+                side, :, pl.ds(first, part)
+            ]
+    for copy in copies:
+        copy.wait()
+    for out, first in ((narrow, 0), (narrow_sent, rows)):
+        out[...] = lax.dot_general(
+            whole[first : first + rows, :],
+            picked[...],
+            (((1,), (1,)), ((), ())),
+            preferred_element_type=jnp.float32,
+        )
+    for load in loads:
+        load.wait()
+    kept[...] = jnp.dot(whole[:rows, :], weights[...], preferred_element_type=jnp.float32)
+    sent[...] = jnp.dot(whole[rows:, :], weights[...], preferred_element_type=jnp.float32).astype(
+        jnp.bfloat16
+    )
+
+
+def run_project(where, down, maps, blocks, backs, column):
     rows, part = blocks[0].shape[0] // 4, blocks[0].shape[1]
     width = column.shape[1]
     free = pl.BlockSpec(memory_space=pl.ANY)
+    one = jax.ShapeDtypeStruct((rows, 2 * maps.shape[0]), jnp.float32)
     return pl.pallas_call(
-        wide_kernel,
-        in_specs=[pl.BlockSpec(memory_space=pltpu.SMEM)] + [free] * 9,
+        project_kernel,
+        in_specs=[pl.BlockSpec(memory_space=pltpu.SMEM)] + [free] * 11,
         out_shape=(
+            one,
+            one,
             jax.ShapeDtypeStruct((rows, width), jnp.float32),
             jax.ShapeDtypeStruct((rows, width), jnp.bfloat16),
         ),
         scratch_shapes=[
             pltpu.VMEM((2 * rows, 16 * part), jnp.bfloat16),
+            pltpu.VMEM((2,) + maps.shape, jnp.bfloat16),
+            pltpu.VMEM((2 * maps.shape[0], 16 * part), jnp.bfloat16),
             pltpu.VMEM((16 * part, width), jnp.bfloat16),
-            pltpu.VMEM((2 * rows, width), jnp.float32),
             pltpu.SemaphoreType.DMA((16,)),
+            pltpu.SemaphoreType.DMA((2,)),
             pltpu.SemaphoreType.DMA((16,)),
         ],
         compiler_params=pltpu.CompilerParams(vmem_limit_bytes=60 * 1024 * 1024),
         cost_estimate=pl.CostEstimate(flops=1 << 31, bytes_accessed=9 << 20, transcendentals=0),
-    )(where, column, *blocks, *backs)
+    )(where, down, maps, *blocks, *backs, column)
 
 
 def per_device(
@@ -269,16 +236,15 @@
     states = lax.all_to_all(states, "req", split_axis=0, concat_axis=0, tiled=True)
     source = lax.dynamic_slice_in_dim(hits[:, 0], here, 1)
 
-    kept, sent = run_narrow(where, w_dt_down.T, w_bc.T, blocks, backs)
-    narrow = kept + lax.ppermute(sent, "req", beside)
-    half, sent = run_wide(where, column, blocks, backs)
+    narrow, narrow_sent, half, sent = run_project(
+        where, w_dt_down.T, w_bc.T, blocks, backs, column
+    )
+    narrow = narrow + lax.ppermute(narrow_sent, "req", beside)
     rest = lax.ppermute(sent, "req", beside)
-
-    low = lax.all_gather(narrow[:32].astype(jnp.bfloat16), "tp", axis=0, tiled=True)
-    spread = jnp.broadcast_to(jnp.transpose(narrow[32:])[:, :, None], (rows, 2 * state_size, 128))
+    low = lax.all_gather(narrow[:, :32].astype(jnp.bfloat16), "tp", axis=1, tiled=True)
+    spread = jnp.broadcast_to(narrow[:, 32:, None], (rows, 2 * state_size, 128))
     step = jax.nn.softplus(
-        lax.dot_general(low, w_dt_up, (((0,), (0,)), ((), ())), preferred_element_type=jnp.float32)
-        + step_bias[None, :]
+        jnp.dot(low, w_dt_up, preferred_element_type=jnp.float32) + step_bias[None, :]
     )
     out, state, squares = run_scan(
         source, half, rest, step, spread, decay_rate, skip_gain[None, :], states, parts

time: 156 us -> 151 us (0.968)
  blocking collectives: 34.1 us -> 31.6 us
  Pallas kernels: 17.9 us -> 15.4 us
    pallas_call x2 -> x1, Pallas kernels: 11.3 us -> 8.84 us  [run_project(): pl.pallas_call(project_kernel, in_specs=[pl.BlockSpec(memory_space=pltpu....]
    all_gather x1, waiting for transfers between devices: 0.02 us -> 1.79 us  [per_device(): lax.all_gather(column, 'req', axis=0, tiled=True, axis_index_groups=along_z)]
    all_gather x1, blocking collectives: 20.7 us -> 19.1 us  [per_device(): lax.all_gather(narrow[:, :32].astype(jnp.bfloat16), 'tp', axis=1, tiled=T...]
  transfers between devices with their start and end apart: 14 -> 14, of which waited for: 6 -> 7; matrix products, arithmetic and copies ran while one was open for 5% -> 6% of each run, Pallas kernels for 7% -> 6%
where the time goes in v3:
time: 151 us; the launch traced here: 150 us
  starting transfers between devices  56.2 us (37%)
  blocking collectives  31.6 us (21%)
  waiting for transfers between devices  21.1 us (14%)
  Pallas kernels  15.4 us (10%)
  between operations  14.4 us (10%)
  local copies, waits for them, and re-layouts  6.71 us (4%)
  other arithmetic  4.23 us (3%)
    ppermute x4, starting transfers between devices, per_device(): blocks.append(lax.ppermute(blocks[-1], 'tp', onward))  19.4 us
    all_gather x1, blocking collectives, per_device(): lax.all_gather(narrow[:, :32].astype(jnp.bfloat16), 'tp', axis=1, tiled=T...  19.1 us
    ppermute x4, waiting for transfers between devices, per_device(): blocks.append(lax.ppermute(blocks[-1], 'tp', onward))  13.1 us
    all_to_all x1, blocking collectives, per_device(): lax.all_to_all(squares, 'tp', split_axis=0, concat_axis=0, tiled=True)  12.4 us
    all_to_all x1, starting transfers between devices, per_device(): lax.all_to_all(states, 'req', split_axis=0, concat_axis=0, tiled=True)  11.2 us
    pallas_call x1, Pallas kernels, run_project(): pl.pallas_call(project_kernel, in_specs=[pl.BlockSpec(memory_space=pltpu....  8.84 us
    ppermute x3, starting transfers between devices, per_device(): backs = [lax.ppermute(block, 'tp', swap) for block in blocks[1:4]]  7.34 us
    ppermute x1, starting transfers between devices, per_device(): lax.ppermute(w_inner, 'req', across)  5.62 us
  transfers between devices with their start and end apart: 14, of which 7 were waited for; matrix products, arithmetic and copies ran while one was open for 6% of the time, Pallas kernels for 6%

profile of v3, /device:TPU:1, one launch (start us, length us, event | category | flops | bytes accessed | tf_op | source)
XLA Modules:
  0.0 150.2 jit_solution(17195333671034740695)
XLA Ops:
  7.2 5.6 %collective-permute-start = (bf16[256,512]{1,0:T(8,128)(2,1)}, bf16[256,512]{1,0:T(8,128)(2,1)S(1)}, u32[]{:S(2)}, u32[]{:S(2)}) collective-permute-start(bf16[256,512]{1,0:T(8,128)(2,1)} %weight.1), channel_id=1, source_target_pairs={{0,32},{16,48},{32,0},{48,16},{64,96},{80,112},{96,64},{112,80},{1... | collective-permute-start | bytes 786440 | tf_op jit(solution)/shard_map/ppermute | solution.py:220
  12.9 1.6 %constant_dynamic-slice_fusion = (bf16[256,256]{1,0:T(8,128)(2,1)S(1)}, bf16[256,256]{1,0:T(8,128)(2,1)}) fusion(bf16[256,512]{1,0:T(8,128)(2,1)} %param.11, s32[]{:T(128)S(6)} %select_n.15, s32[]{:T(128)S(6)} %select_n.14), kind=kLoop, calls=%fused_computation.10 | loop fusion | bytes 524296 | tf_op jit(solution)/shard_map/dynamic_slice | solution.py:218
  14.5 2.2 %collective-permute-start.1 = (bf16[256,256]{1,0:T(8,128)(2,1)S(1)}, bf16[256,256]{1,0:T(8,128)(2,1)S(1)}, u32[]{:S(2)}, u32[]{:S(2)}) collective-permute-start(bf16[256,256]{1,0:T(8,128)(2,1)S(1)} %get-tuple-element.20), channel_id=1, source_target_pairs={{0,16},{16,0},{32,48},{48,32},{64,80},{80,64},{96,112},{112,96},{1... | collective-permute-start | bytes 393224 | tf_op jit(solution)/shard_map/ppermute | solution.py:220
  16.7 4.9 %collective-permute-done.1.more_token = bf16[256,256]{1,0:T(8,128)(2,1)S(1)} collective-permute-done((bf16[256,256]{1,0:T(8,128)(2,1)S(1)}, bf16[256,256]{1,0:T(8,128)(2,1)S(1)}, u32[]{:S(2)}, u32[]{:S(2)}) %collective-permute-start.1) | collective-permute-done | bytes 131104 | tf_op jit(solution)/shard_map/ppermute | solution.py:220
  22.4 2.0 %shard_map.122 = (bf16[512,512]{1,0:T(8,128)(2,1)}, bf16[512,256]{1,0:T(8,128)(2,1)}) custom-call(bf16[256,512]{1,0:T(8,128)(2,1)} %weight.1, bf16[256,512]{1,0:T(8,128)(2,1)} %copy-done.8, bf16[256,256]{1,0:T(8,128)(2,1)} %get-tuple-element.21.token, bf16[256,256]{1,0:T(8,128)(2,1)} %copy-done.9), custom_call_target="tpu_custom_call" | custom-call | bytes 2097152 | tf_op jit(solution)/shard_map/pallas_call | solution.py:93
  24.4 5.0 %collective-permute-start.2 = (bf16[512,256]{1,0:T(8,128)(2,1)}, bf16[512,256]{1,0:T(8,128)(2,1)S(1)}, u32[]{:S(2)}, u32[]{:S(2)}) collective-permute-start(bf16[512,256]{1,0:T(8,128)(2,1)} %get-tuple-element.11), channel_id=1, source_target_pairs={{0,1},{1,0},{2,3},{3,2},{4,5},{5,4},{6,7},{7,6},{8,9},{9,8},{10,11... | collective-permute-start | bytes 786440 | tf_op jit(solution)/shard_map/ppermute | solution.py:225
  30.8 3.8 %collective-permute-start.3 = (bf16[1024,256]{1,0:T(8,128)(2,1)S(1)}, bf16[1024,256]{1,0:T(8,128)(2,1)S(1)}, u32[]{:S(2)}, u32[]{:S(2)}) collective-permute-start(bf16[1024,256]{1,0:T(8,128)(2,1)S(1)} %constant_dynamic-update-slice_fusion.rest_0_), channel_id=1, source_target_pairs={{0,2},{1,15},{2,4},{3,1},{4,6},{5,3},{6,8},{7,5},{8,10},{9,7},{10,... | collective-permute-start | bytes 1572872 | tf_op jit(solution)/shard_map/ppermute | solution.py:227
  34.6 6.4 %collective-permute-done.3.rest_1_ = bf16[1024,256]{1,0:T(8,128)(2,1)S(1)} collective-permute-done((bf16[1024,256]{1,0:T(8,128)(2,1)S(1)}, bf16[1024,256]{1,0:T(8,128)(2,1)S(1)}, u32[]{:S(2)}, u32[]{:S(2)}) %collective-permute-start.3) | collective-permute-done | bytes 524320 | tf_op jit(solution)/shard_map/ppermute | solution.py:227
  41.0 4.8 %collective-permute-start.4 = (bf16[1024,256]{1,0:T(8,128)(2,1)S(1)}, bf16[1024,256]{1,0:T(8,128)(2,1)S(1)}, u32[]{:S(2)}, u32[]{:S(2)}) collective-permute-start(bf16[1024,256]{1,0:T(8,128)(2,1)S(1)} %collective-permute-done.3.rest_1_), channel_id=1, source_target_pairs={{0,2},{1,15},{2,4},{3,1},{4,6},{5,3},{6,8},{7,5},{8,10},{9,7},{10,... | collective-permute-start | bytes 1572872 | tf_op jit(solution)/shard_map/ppermute | solution.py:227
  45.8 6.1 %collective-permute-done.4.rest_2_ = bf16[1024,256]{1,0:T(8,128)(2,1)S(1)} collective-permute-done((bf16[1024,256]{1,0:T(8,128)(2,1)S(1)}, bf16[1024,256]{1,0:T(8,128)(2,1)S(1)}, u32[]{:S(2)}, u32[]{:S(2)}) %collective-permute-start.4) | collective-permute-done | bytes 524320 | tf_op jit(solution)/shard_map/ppermute | solution.py:227
  51.9 5.4 %collective-permute-start.5 = (bf16[1024,256]{1,0:T(8,128)(2,1)S(1)}, bf16[1024,256]{1,0:T(8,128)(2,1)S(1)}, u32[]{:S(2)}, u32[]{:S(2)}) collective-permute-start(bf16[1024,256]{1,0:T(8,128)(2,1)S(1)} %collective-permute-done.4.rest_2_), channel_id=1, source_target_pairs={{0,2},{1,15},{2,4},{3,1},{4,6},{5,3},{6,8},{7,5},{8,10},{9,7},{10,... | collective-permute-start | bytes 1572872 | tf_op jit(solution)/shard_map/ppermute | solution.py:227
  58.4 2.3 %collective-permute-start.7 = (bf16[1024,256]{1,0:T(8,128)(2,1)S(1)}, bf16[1024,256]{1,0:T(8,128)(2,1)}, u32[]{:S(2)}, u32[]{:S(2)}) collective-permute-start(bf16[1024,256]{1,0:T(8,128)(2,1)S(1)} %collective-permute-done.3.rest_1_), channel_id=1, source_target_pairs={{0,1},{1,0},{2,3},{3,2},{4,5},{5,4},{6,7},{7,6},{8,9},{9,8},{10,11... | collective-permute-start | bytes 1572872 | tf_op jit(solution)/shard_map/ppermute | solution.py:228
  60.6 2.1 %collective-permute-start.8 = (bf16[1024,256]{1,0:T(8,128)(2,1)S(1)}, bf16[1024,256]{1,0:T(8,128)(2,1)}, u32[]{:S(2)}, u32[]{:S(2)}) collective-permute-start(bf16[1024,256]{1,0:T(8,128)(2,1)S(1)} %collective-permute-done.4.rest_2_), channel_id=1, source_target_pairs={{0,1},{1,0},{2,3},{3,2},{4,5},{5,4},{6,7},{7,6},{8,9},{9,8},{10,11... | collective-permute-start | bytes 1572872 | tf_op jit(solution)/shard_map/ppermute | solution.py:228
  63.4 5.4 %collective-permute-start.6 = (bf16[1024,256]{1,0:T(8,128)(2,1)S(1)}, bf16[1024,256]{1,0:T(8,128)(2,1)}, u32[]{:S(2)}, u32[]{:S(2)}) collective-permute-start(bf16[1024,256]{1,0:T(8,128)(2,1)S(1)} %collective-permute-done.5.rest_3_), channel_id=1, source_target_pairs={{0,2},{1,15},{2,4},{3,1},{4,6},{5,3},{6,8},{7,5},{8,10},{9,7},{10,... | collective-permute-start | bytes 1572872 | tf_op jit(solution)/shard_map/ppermute | solution.py:227
  68.8 3.0 %collective-permute-start.9 = (bf16[1024,256]{1,0:T(8,128)(2,1)S(1)}, bf16[1024,256]{1,0:T(8,128)(2,1)}, u32[]{:S(2)}, u32[]{:S(2)}) collective-permute-start(bf16[1024,256]{1,0:T(8,128)(2,1)S(1)} %collective-permute-done.5.rest_3_), channel_id=1, source_target_pairs={{0,1},{1,0},{2,3},{3,2},{4,5},{5,4},{6,7},{7,6},{8,9},{9,8},{10,11... | collective-permute-start | bytes 1572872 | tf_op jit(solution)/shard_map/ppermute | solution.py:228
  72.6 1.4 gather_fusion
  74.0 11.2 %all-to-all-start = ((bf16[32,16,512]{2,1,0:T(8,128)(2,1)}), bf16[32,16,512]{2,1,0:T(8,128)(2,1)S(1)}, u32[]{:S(2)}, u32[]{:S(2)}) async-start(bf16[32,16,512]{2,1,0:T(8,128)(2,1)} %gather_fusion), calls=%async_computation | async-start | bytes 1048576 | tf_op jit(solution)/shard_map/all_to_all | solution.py:236
  85.8 1.8 %all-gather.2.cloned.1.call-done.rest_8_ = bf16[4096,512]{1,0:T(8,128)(2,1)} async-done(((bf16[512,512]{1,0:T(8,128)(2,1)}), bf16[4096,512]{1,0:T(8,128)(2,1)}) %all-gather.2.cloned.1.call-update) | async-done | bytes 4194320 | tf_op jit(solution)/shard_map/all_gather | solution.py:223
  87.6 8.8 %shard_map.123 = (f32[256,64]{1,0:T(8,128)}, f32[256,64]{1,0:T(8,128)}, f32[256,512]{1,0:T(8,128)}, bf16[256,512]{1,0:T(8,128)(2,1)}) custom-call(s32[32]{0:T(128)} %pad_add_fusion.where, bf16[32,8192]{1,0:T(8,128)(2,1)} %bitcast.14, bf16[32,8192]{1,0:T(8,128)(2,1)} %bitcast.15, bf16[1024,256]{1,0:T(8,128)(2,1)} %copy-done.4, bf16[1024,256]{1,0:T(8,128)(2,1)} %copy-done.5, ...), custom_call_target="tpu_custom_call" | custom-call | flops 2147483648 | bytes 9437184 | tf_op jit(solution)/shard_map/pallas_call | solution.py:164
  96.5 3.2 %collective-permute-start.11 = (f32[256,64]{1,0:T(8,128)}, f32[256,64]{1,0:T(8,128)S(1)}, u32[]{:S(2)}, u32[]{:S(2)}) collective-permute-start(f32[256,64]{1,0:T(8,128)} %get-tuple-element.16), channel_id=1, source_target_pairs={{0,16},{16,0},{32,48},{48,32},{64,80},{80,64},{96,112},{112,96},{1... | collective-permute-start | bytes 196616 | tf_op jit(solution)/shard_map/ppermute | solution.py:242
  100.3 2.2 %collective-permute-start.10 = (bf16[256,512]{1,0:T(8,128)(2,1)}, bf16[256,512]{1,0:T(8,128)(2,1)S(1)}, u32[]{:S(2)}, u32[]{:S(2)}) collective-permute-start(bf16[256,512]{1,0:T(8,128)(2,1)} %get-tuple-element.14), channel_id=1, source_target_pairs={{0,16},{16,0},{32,48},{48,32},{64,80},{80,64},{96,112},{112,96},{1... | collective-permute-start | bytes 786440 | tf_op jit(solution)/shard_map/ppermute | solution.py:243
  104.4 19.1 %all_gather.7 = bf16[256,512]{0,1:T(8,128)(2,1)S(1)} all-gather(bf16[256,32]{0,1:T(8,128)(2,1)S(1)} %copy.13), channel_id=1, replica_groups=mesh['req'=32,'tp'=16] {'tp'}, dimensions={1}, use_global_device_ids=true | all-gather | bytes 278528 | tf_op jit(solution)/shard_map/all_gather | solution.py:244
  125.4 4.6 %shard_map.124 = (f32[256,512]{1,0:T(8,128)S(1)}, f32[16,512]{1,0:T(8,128)}, f32[16,256]{1,0:T(8,128)S(1)}) custom-call(s32[1]{0:T(128)} %bitcast.source, f32[256,512]{1,0:T(8,128)S(1)} %copy-done.1, bf16[256,512]{1,0:T(8,128)(2,1)S(1)} %collective-permute-done.10.rest, f32[256,512]{1,0:T(8,128)S(1)} %compare_select_fusion.steps, ...), custom_call_target="tpu_custom_call" | custom-call | flops 16777216 | bytes 8388608 | tf_op jit(solution)/shard_map/pallas_call | solution.py:64
  130.0 12.4 %all_to_all.14 = f32[16,1,256]{2,1,0:T(1,128)S(1)} all-to-all(f32[16,1,256]{2,1,0:T(1,128)S(1)} %copy.14), channel_id=1, replica_groups=mesh['req'=32,'tp'=16] {'tp'}, dimensions={0} | all-to-all | bytes 32768 | tf_op jit(solution)/shard_map/all_to_all | solution.py:252
  (54 shorter events, 10.5 us)
Async XLA Ops:
  7.2 116.5 %copy-start = (bf16[512,512]{1,0:T(8,128)(2,1)S(1)}, bf16[512,512]{1,0:T(8,128)(2,1)}, u32[]{:S(2)}) copy-start(bf16[512,512]{1,0:T(8,128)(2,1)} %param.15) | copy-start | bytes 1572868
  7.2 80.4 %all-gather.2.cloned.1.call-start = ((), (), s32[]{:S(2)}) async-start(), calls=%async_computation.2 | async-start | bytes 4718592 | tf_op jit(solution)/shard_map/all_gather | solution.py:223
  7.2 14.4 %collective-permute-start = (bf16[256,512]{1,0:T(8,128)(2,1)}, bf16[256,512]{1,0:T(8,128)(2,1)S(1)}, u32[]{:S(2)}, u32[]{:S(2)}) collective-permute-start(bf16[256,512]{1,0:T(8,128)(2,1)} %weight.1), channel_id=1, source_target_pairs={{0,32},{16,48},{32,0},{48,16},{64,96},{80,112},{96,64},{112,80},{1... | collective-permute-start | bytes 786440 | tf_op jit(solution)/shard_map/ppermute | solution.py:220
  14.5 7.1 %collective-permute-start.1 = (bf16[256,256]{1,0:T(8,128)(2,1)S(1)}, bf16[256,256]{1,0:T(8,128)(2,1)S(1)}, u32[]{:S(2)}, u32[]{:S(2)}) collective-permute-start(bf16[256,256]{1,0:T(8,128)(2,1)S(1)} %get-tuple-element.20), channel_id=1, source_target_pairs={{0,16},{16,0},{32,48},{48,32},{64,80},{80,64},{96,112},{112,96},{1... | collective-permute-start | bytes 393224 | tf_op jit(solution)/shard_map/ppermute | solution.py:220
  24.4 6.3 %collective-permute-start.2 = (bf16[512,256]{1,0:T(8,128)(2,1)}, bf16[512,256]{1,0:T(8,128)(2,1)S(1)}, u32[]{:S(2)}, u32[]{:S(2)}) collective-permute-start(bf16[512,256]{1,0:T(8,128)(2,1)} %get-tuple-element.11), channel_id=1, source_target_pairs={{0,1},{1,0},{2,3},{3,2},{4,5},{5,4},{6,7},{7,6},{8,9},{9,8},{10,11... | collective-permute-start | bytes 786440 | tf_op jit(solution)/shard_map/ppermute | solution.py:225
  30.8 56.8 %copy-start.4 = (bf16[1024,256]{1,0:T(8,128)(2,1)}, bf16[1024,256]{1,0:T(8,128)(2,1)S(1)}, u32[]{:S(2)}) copy-start(bf16[1024,256]{1,0:T(8,128)(2,1)S(1)} %constant_dynamic-update-slice_fusion.rest_0_) | copy-start | bytes 1572868
  30.8 10.2 %collective-permute-start.3 = (bf16[1024,256]{1,0:T(8,128)(2,1)S(1)}, bf16[1024,256]{1,0:T(8,128)(2,1)S(1)}, u32[]{:S(2)}, u32[]{:S(2)}) collective-permute-start(bf16[1024,256]{1,0:T(8,128)(2,1)S(1)} %constant_dynamic-update-slice_fusion.rest_0_), channel_id=1, source_target_pairs={{0,2},{1,15},{2,4},{3,1},{4,6},{5,3},{6,8},{7,5},{8,10},{9,7},{10,... | collective-permute-start | bytes 1572872 | tf_op jit(solution)/shard_map/ppermute | solution.py:227
  41.0 46.6 %copy-start.5 = (bf16[1024,256]{1,0:T(8,128)(2,1)}, bf16[1024,256]{1,0:T(8,128)(2,1)S(1)}, u32[]{:S(2)}) copy-start(bf16[1024,256]{1,0:T(8,128)(2,1)S(1)} %collective-permute-done.3.rest_1_) | copy-start | bytes 1572868
  41.0 10.9 %collective-permute-start.4 = (bf16[1024,256]{1,0:T(8,128)(2,1)S(1)}, bf16[1024,256]{1,0:T(8,128)(2,1)S(1)}, u32[]{:S(2)}, u32[]{:S(2)}) collective-permute-start(bf16[1024,256]{1,0:T(8,128)(2,1)S(1)} %collective-permute-done.3.rest_1_), channel_id=1, source_target_pairs={{0,2},{1,15},{2,4},{3,1},{4,6},{5,3},{6,8},{7,5},{8,10},{9,7},{10,... | collective-permute-start | bytes 1572872 | tf_op jit(solution)/shard_map/ppermute | solution.py:227
  51.9 35.8 %copy-start.6 = (bf16[1024,256]{1,0:T(8,128)(2,1)}, bf16[1024,256]{1,0:T(8,128)(2,1)S(1)}, u32[]{:S(2)}) copy-start(bf16[1024,256]{1,0:T(8,128)(2,1)S(1)} %collective-permute-done.4.rest_2_) | copy-start | bytes 1572868
  51.9 11.5 %collective-permute-start.5 = (bf16[1024,256]{1,0:T(8,128)(2,1)S(1)}, bf16[1024,256]{1,0:T(8,128)(2,1)S(1)}, u32[]{:S(2)}, u32[]{:S(2)}) collective-permute-start(bf16[1024,256]{1,0:T(8,128)(2,1)S(1)} %collective-permute-done.4.rest_2_), channel_id=1, source_target_pairs={{0,2},{1,15},{2,4},{3,1},{4,6},{5,3},{6,8},{7,5},{8,10},{9,7},{10,... | collective-permute-start | bytes 1572872 | tf_op jit(solution)/shard_map/ppermute | solution.py:227
  58.4 27.4 %collective-permute-start.7 = (bf16[1024,256]{1,0:T(8,128)(2,1)S(1)}, bf16[1024,256]{1,0:T(8,128)(2,1)}, u32[]{:S(2)}, u32[]{:S(2)}) collective-permute-start(bf16[1024,256]{1,0:T(8,128)(2,1)S(1)} %collective-permute-done.3.rest_1_), channel_id=1, source_target_pairs={{0,1},{1,0},{2,3},{3,2},{4,5},{5,4},{6,7},{7,6},{8,9},{9,8},{10,11... | collective-permute-start | bytes 1572872 | tf_op jit(solution)/shard_map/ppermute | solution.py:228
  60.6 25.2 %collective-permute-start.8 = (bf16[1024,256]{1,0:T(8,128)(2,1)S(1)}, bf16[1024,256]{1,0:T(8,128)(2,1)}, u32[]{:S(2)}, u32[]{:S(2)}) collective-permute-start(bf16[1024,256]{1,0:T(8,128)(2,1)S(1)} %collective-permute-done.4.rest_2_), channel_id=1, source_target_pairs={{0,1},{1,0},{2,3},{3,2},{4,5},{5,4},{6,7},{7,6},{8,9},{9,8},{10,11... | collective-permute-start | bytes 1572872 | tf_op jit(solution)/shard_map/ppermute | solution.py:228
  63.4 24.2 %copy-start.7 = (bf16[1024,256]{1,0:T(8,128)(2,1)}, bf16[1024,256]{1,0:T(8,128)(2,1)S(1)}, u32[]{:S(2)}) copy-start(bf16[1024,256]{1,0:T(8,128)(2,1)S(1)} %collective-permute-done.5.rest_3_) | copy-start | bytes 1572868
  63.4 22.4 %collective-permute-start.6 = (bf16[1024,256]{1,0:T(8,128)(2,1)S(1)}, bf16[1024,256]{1,0:T(8,128)(2,1)}, u32[]{:S(2)}, u32[]{:S(2)}) collective-permute-start(bf16[1024,256]{1,0:T(8,128)(2,1)S(1)} %collective-permute-done.5.rest_3_), channel_id=1, source_target_pairs={{0,2},{1,15},{2,4},{3,1},{4,6},{5,3},{6,8},{7,5},{8,10},{9,7},{10,... | collective-permute-start | bytes 1572872 | tf_op jit(solution)/shard_map/ppermute | solution.py:227
  68.8 17.0 %collective-permute-start.9 = (bf16[1024,256]{1,0:T(8,128)(2,1)S(1)}, bf16[1024,256]{1,0:T(8,128)(2,1)}, u32[]{:S(2)}, u32[]{:S(2)}) collective-permute-start(bf16[1024,256]{1,0:T(8,128)(2,1)S(1)} %collective-permute-done.5.rest_3_), channel_id=1, source_target_pairs={{0,1},{1,0},{2,3},{3,2},{4,5},{5,4},{6,7},{7,6},{8,9},{9,8},{10,11... | collective-permute-start | bytes 1572872 | tf_op jit(solution)/shard_map/ppermute | solution.py:228
  74.0 50.2 %all-to-all-start = ((bf16[32,16,512]{2,1,0:T(8,128)(2,1)}), bf16[32,16,512]{2,1,0:T(8,128)(2,1)S(1)}, u32[]{:S(2)}, u32[]{:S(2)}) async-start(bf16[32,16,512]{2,1,0:T(8,128)(2,1)} %gather_fusion), calls=%async_computation | async-start | bytes 1048576 | tf_op jit(solution)/shard_map/all_to_all | solution.py:236
  87.6 36.0 %copy-start.11 = (f32[512]{0:T(512)S(1)}, f32[512]{0:T(512)}, u32[]{:S(2)}) copy-start(f32[512]{0:T(512)} %param.16) | copy-start | bytes 6148
  96.5 28.9 %copy-start.1 = (f32[256,512]{1,0:T(8,128)S(1)}, f32[256,512]{1,0:T(8,128)}, u32[]{:S(2)}) copy-start(f32[256,512]{1,0:T(8,128)} %get-tuple-element.13.half) | copy-start | bytes 1572868
  96.5 28.9 %copy-start.2 = (f32[16,512]{1,0:T(8,128)S(1)}, f32[16,512]{1,0:T(8,128)}, u32[]{:S(2)}) copy-start(f32[16,512]{1,0:T(8,128)} %decay.1) | copy-start | bytes 98308
  96.5 28.9 %copy-start.3 = (f32[512]{0:T(512)S(1)}, f32[512]{0:T(512)}, u32[]{:S(2)}) copy-start(f32[512]{0:T(512)} %param.18) | copy-start | bytes 6148
  96.5 6.9 %collective-permute-start.11 = (f32[256,64]{1,0:T(8,128)}, f32[256,64]{1,0:T(8,128)S(1)}, u32[]{:S(2)}, u32[]{:S(2)}) collective-permute-start(f32[256,64]{1,0:T(8,128)} %get-tuple-element.16), channel_id=1, source_target_pairs={{0,16},{16,0},{32,48},{48,32},{64,80},{80,64},{96,112},{112,96},{1... | collective-permute-start | bytes 196616 | tf_op jit(solution)/shard_map/ppermute | solution.py:242
  100.3 23.9 %collective-permute-start.10 = (bf16[256,512]{1,0:T(8,128)(2,1)}, bf16[256,512]{1,0:T(8,128)(2,1)S(1)}, u32[]{:S(2)}, u32[]{:S(2)}) collective-permute-start(bf16[256,512]{1,0:T(8,128)(2,1)} %get-tuple-element.14), channel_id=1, source_target_pairs={{0,16},{16,0},{32,48},{48,32},{64,80},{80,64},{96,112},{112,96},{1... | collective-permute-start | bytes 786440 | tf_op jit(solution)/shard_map/ppermute | solution.py:243
  124.2 18.3 %copy-start.10 = (f32[512]{0:T(512)S(1)}, f32[512]{0:T(512)}, u32[]{:S(2)}) copy-start(f32[512]{0:T(512)} %param.19) | copy-start | bytes 6148
  (2 other events, 1.4 us)
Sparse Core Ops, SparseCore 0:
  24.5 63.0 all-gather.1

commit v4 on v3

--- a/solution.py
+++ b/solution.py
@@ -115,7 +115,7 @@
 
 def project_kernel(where, down, maps, *rest):
     blocks, backs, column = rest[:5], rest[5:8], rest[8]
-    narrow, narrow_sent, kept, sent, whole, thin, picked, weights, landed, taken, loaded = rest[9:]
+    narrow, narrow_sent, kept, sent, whole, thin, picked, weights, total, landed, taken, loaded = rest[9:]
     part = blocks[0].shape[1]
     rows = kept.shape[0]
     size = maps.shape[0]
@@ -129,8 +129,21 @@
         )
         for at in range(16)
     ]
-    for copy in takes + copies + loads:
-        copy.start()
+    for first in range(0, 16, 8):
+        for copy in copies[first : first + 8] + loads[first : first + 8]:
+            copy.start()
+    for take in takes:
+        take.start()
+    for copy in copies[:8] + loads[:8]:
+        copy.wait()
+    span = 8 * part
+    kept[...] = jnp.dot(whole[:rows, :span], weights[:span, :], preferred_element_type=jnp.float32)
+    total[...] = jnp.dot(whole[rows:, :span], weights[:span, :], preferred_element_type=jnp.float32)
+    for copy in copies[8:] + loads[8:]:
+        copy.wait()
+    kept[...] += jnp.dot(whole[:rows, span:], weights[span:, :], preferred_element_type=jnp.float32)
+    more = jnp.dot(whole[rows:, span:], weights[span:, :], preferred_element_type=jnp.float32)
+    sent[...] = (total[...] + more).astype(jnp.bfloat16)
     for take in takes:
         take.wait()
     for at in range(16):
@@ -139,8 +152,6 @@
             picked[side * size : (side + 1) * size, at * part : (at + 1) * part] = thin[
                 side, :, pl.ds(first, part)
             ]
-    for copy in copies:
-        copy.wait()
     for out, first in ((narrow, 0), (narrow_sent, rows)):
         out[...] = lax.dot_general(
             whole[first : first + rows, :],
@@ -148,12 +159,6 @@
             (((1,), (1,)), ((), ())),
             preferred_element_type=jnp.float32,
         )
-    for load in loads:
-        load.wait()
-    kept[...] = jnp.dot(whole[:rows, :], weights[...], preferred_element_type=jnp.float32)
-    sent[...] = jnp.dot(whole[rows:, :], weights[...], preferred_element_type=jnp.float32).astype(
-        jnp.bfloat16
-    )
 
 
 def run_project(where, down, maps, blocks, backs, column):
@@ -175,6 +180,7 @@
             pltpu.VMEM((2,) + maps.shape, jnp.bfloat16),
             pltpu.VMEM((2 * maps.shape[0], 16 * part), jnp.bfloat16),
             pltpu.VMEM((16 * part, width), jnp.bfloat16),
+            pltpu.VMEM((rows, width), jnp.float32),
             pltpu.SemaphoreType.DMA((16,)),
             pltpu.SemaphoreType.DMA((2,)),
             pltpu.SemaphoreType.DMA((16,)),

time: 151 us -> 151 us (level)
  transfers between devices with their start and end apart: 14 -> 14, of which waited for: 7 -> 7; matrix products, arithmetic and copies ran while one was open for 6% -> 6% of each run, Pallas kernels for 6% -> 5%
where the time goes in v4:
time: 151 us; the launch traced here: 150 us
  starting transfers between devices  56.2 us (37%)
  blocking collectives  32.3 us (21%)
  waiting for transfers between devices  21.1 us (14%)
  Pallas kernels  14.5 us (10%)
  between operations  14.4 us (10%)
  local copies, waits for them, and re-layouts  6.71 us (4%)
  other arithmetic  4.23 us (3%)
    ppermute x4, starting transfers between devices, per_device(): blocks.append(lax.ppermute(blocks[-1], 'tp', onward))  19.4 us
    all_gather x1, blocking collectives, per_device(): lax.all_gather(narrow[:, :32].astype(jnp.bfloat16), 'tp', axis=1, tiled=T...  19.2 us
    ppermute x4, waiting for transfers between devices, per_device(): blocks.append(lax.ppermute(blocks[-1], 'tp', onward))  13.1 us
    all_to_all x1, blocking collectives, per_device(): lax.all_to_all(squares, 'tp', split_axis=0, concat_axis=0, tiled=True)  13.1 us
    all_to_all x1, starting transfers between devices, per_device(): lax.all_to_all(states, 'req', split_axis=0, concat_axis=0, tiled=True)  11.2 us
    pallas_call x1, Pallas kernels, run_project(): pl.pallas_call(project_kernel, in_specs=[pl.BlockSpec(memory_space=pltpu....  7.86 us
    ppermute x3, starting transfers between devices, per_device(): backs = [lax.ppermute(block, 'tp', swap) for block in blocks[1:4]]  7.34 us
    ppermute x1, starting transfers between devices, per_device(): lax.ppermute(w_inner, 'req', across)  5.62 us
  transfers between devices with their start and end apart: 14, of which 7 were waited for; matrix products, arithmetic and copies ran while one was open for 6% of the time, Pallas kernels for 5%

profile of v4, /device:TPU:1, one launch (start us, length us, event | category | flops | bytes accessed | tf_op | source)
XLA Modules:
  0.0 149.8 jit_solution(17773582862120840484)
XLA Ops:
  7.2 5.6 %collective-permute-start = (bf16[256,512]{1,0:T(8,128)(2,1)}, bf16[256,512]{1,0:T(8,128)(2,1)S(1)}, u32[]{:S(2)}, u32[]{:S(2)}) collective-permute-start(bf16[256,512]{1,0:T(8,128)(2,1)} %weight.1), channel_id=1, source_target_pairs={{0,32},{16,48},{32,0},{48,16},{64,96},{80,112},{96,64},{112,80},{1... | collective-permute-start | bytes 786440 | tf_op jit(solution)/shard_map/ppermute | solution.py:226
  12.9 1.6 %constant_dynamic-slice_fusion = (bf16[256,256]{1,0:T(8,128)(2,1)S(1)}, bf16[256,256]{1,0:T(8,128)(2,1)}) fusion(bf16[256,512]{1,0:T(8,128)(2,1)} %param.11, s32[]{:T(128)S(6)} %select_n.15, s32[]{:T(128)S(6)} %select_n.14), kind=kLoop, calls=%fused_computation.10 | loop fusion | bytes 524296 | tf_op jit(solution)/shard_map/dynamic_slice | solution.py:224
  14.5 2.2 %collective-permute-start.1 = (bf16[256,256]{1,0:T(8,128)(2,1)S(1)}, bf16[256,256]{1,0:T(8,128)(2,1)S(1)}, u32[]{:S(2)}, u32[]{:S(2)}) collective-permute-start(bf16[256,256]{1,0:T(8,128)(2,1)S(1)} %get-tuple-element.20), channel_id=1, source_target_pairs={{0,16},{16,0},{32,48},{48,32},{64,80},{80,64},{96,112},{112,96},{1... | collective-permute-start | bytes 393224 | tf_op jit(solution)/shard_map/ppermute | solution.py:226
  16.7 4.9 %collective-permute-done.1.more_token = bf16[256,256]{1,0:T(8,128)(2,1)S(1)} collective-permute-done((bf16[256,256]{1,0:T(8,128)(2,1)S(1)}, bf16[256,256]{1,0:T(8,128)(2,1)S(1)}, u32[]{:S(2)}, u32[]{:S(2)}) %collective-permute-start.1) | collective-permute-done | bytes 131104 | tf_op jit(solution)/shard_map/ppermute | solution.py:226
  22.4 2.0 %shard_map.122 = (bf16[512,512]{1,0:T(8,128)(2,1)}, bf16[512,256]{1,0:T(8,128)(2,1)}) custom-call(bf16[256,512]{1,0:T(8,128)(2,1)} %weight.1, bf16[256,512]{1,0:T(8,128)(2,1)} %copy-done.8, bf16[256,256]{1,0:T(8,128)(2,1)} %get-tuple-element.21.token, bf16[256,256]{1,0:T(8,128)(2,1)} %copy-done.9), custom_call_target="tpu_custom_call" | custom-call | bytes 2097152 | tf_op jit(solution)/shard_map/pallas_call | solution.py:93
  24.4 5.0 %collective-permute-start.2 = (bf16[512,256]{1,0:T(8,128)(2,1)}, bf16[512,256]{1,0:T(8,128)(2,1)S(1)}, u32[]{:S(2)}, u32[]{:S(2)}) collective-permute-start(bf16[512,256]{1,0:T(8,128)(2,1)} %get-tuple-element.11), channel_id=1, source_target_pairs={{0,1},{1,0},{2,3},{3,2},{4,5},{5,4},{6,7},{7,6},{8,9},{9,8},{10,11... | collective-permute-start | bytes 786440 | tf_op jit(solution)/shard_map/ppermute | solution.py:231
  30.8 3.8 %collective-permute-start.3 = (bf16[1024,256]{1,0:T(8,128)(2,1)S(1)}, bf16[1024,256]{1,0:T(8,128)(2,1)S(1)}, u32[]{:S(2)}, u32[]{:S(2)}) collective-permute-start(bf16[1024,256]{1,0:T(8,128)(2,1)S(1)} %constant_dynamic-update-slice_fusion.rest_0_), channel_id=1, source_target_pairs={{0,2},{1,15},{2,4},{3,1},{4,6},{5,3},{6,8},{7,5},{8,10},{9,7},{10,... | collective-permute-start | bytes 1572872 | tf_op jit(solution)/shard_map/ppermute | solution.py:233
  34.6 6.4 %collective-permute-done.3.rest_1_ = bf16[1024,256]{1,0:T(8,128)(2,1)S(1)} collective-permute-done((bf16[1024,256]{1,0:T(8,128)(2,1)S(1)}, bf16[1024,256]{1,0:T(8,128)(2,1)S(1)}, u32[]{:S(2)}, u32[]{:S(2)}) %collective-permute-start.3) | collective-permute-done | bytes 524320 | tf_op jit(solution)/shard_map/ppermute | solution.py:233
  41.0 4.8 %collective-permute-start.4 = (bf16[1024,256]{1,0:T(8,128)(2,1)S(1)}, bf16[1024,256]{1,0:T(8,128)(2,1)S(1)}, u32[]{:S(2)}, u32[]{:S(2)}) collective-permute-start(bf16[1024,256]{1,0:T(8,128)(2,1)S(1)} %collective-permute-done.3.rest_1_), channel_id=1, source_target_pairs={{0,2},{1,15},{2,4},{3,1},{4,6},{5,3},{6,8},{7,5},{8,10},{9,7},{10,... | collective-permute-start | bytes 1572872 | tf_op jit(solution)/shard_map/ppermute | solution.py:233
  45.8 6.1 %collective-permute-done.4.rest_2_ = bf16[1024,256]{1,0:T(8,128)(2,1)S(1)} collective-permute-done((bf16[1024,256]{1,0:T(8,128)(2,1)S(1)}, bf16[1024,256]{1,0:T(8,128)(2,1)S(1)}, u32[]{:S(2)}, u32[]{:S(2)}) %collective-permute-start.4) | collective-permute-done | bytes 524320 | tf_op jit(solution)/shard_map/ppermute | solution.py:233
  51.9 5.4 %collective-permute-start.5 = (bf16[1024,256]{1,0:T(8,128)(2,1)S(1)}, bf16[1024,256]{1,0:T(8,128)(2,1)S(1)}, u32[]{:S(2)}, u32[]{:S(2)}) collective-permute-start(bf16[1024,256]{1,0:T(8,128)(2,1)S(1)} %collective-permute-done.4.rest_2_), channel_id=1, source_target_pairs={{0,2},{1,15},{2,4},{3,1},{4,6},{5,3},{6,8},{7,5},{8,10},{9,7},{10,... | collective-permute-start | bytes 1572872 | tf_op jit(solution)/shard_map/ppermute | solution.py:233
  58.4 2.3 %collective-permute-start.7 = (bf16[1024,256]{1,0:T(8,128)(2,1)S(1)}, bf16[1024,256]{1,0:T(8,128)(2,1)}, u32[]{:S(2)}, u32[]{:S(2)}) collective-permute-start(bf16[1024,256]{1,0:T(8,128)(2,1)S(1)} %collective-permute-done.3.rest_1_), channel_id=1, source_target_pairs={{0,1},{1,0},{2,3},{3,2},{4,5},{5,4},{6,7},{7,6},{8,9},{9,8},{10,11... | collective-permute-start | bytes 1572872 | tf_op jit(solution)/shard_map/ppermute | solution.py:234
  60.6 2.1 %collective-permute-start.8 = (bf16[1024,256]{1,0:T(8,128)(2,1)S(1)}, bf16[1024,256]{1,0:T(8,128)(2,1)}, u32[]{:S(2)}, u32[]{:S(2)}) collective-permute-start(bf16[1024,256]{1,0:T(8,128)(2,1)S(1)} %collective-permute-done.4.rest_2_), channel_id=1, source_target_pairs={{0,1},{1,0},{2,3},{3,2},{4,5},{5,4},{6,7},{7,6},{8,9},{9,8},{10,11... | collective-permute-start | bytes 1572872 | tf_op jit(solution)/shard_map/ppermute | solution.py:234
  63.4 5.4 %collective-permute-start.6 = (bf16[1024,256]{1,0:T(8,128)(2,1)S(1)}, bf16[1024,256]{1,0:T(8,128)(2,1)}, u32[]{:S(2)}, u32[]{:S(2)}) collective-permute-start(bf16[1024,256]{1,0:T(8,128)(2,1)S(1)} %collective-permute-done.5.rest_3_), channel_id=1, source_target_pairs={{0,2},{1,15},{2,4},{3,1},{4,6},{5,3},{6,8},{7,5},{8,10},{9,7},{10,... | collective-permute-start | bytes 1572872 | tf_op jit(solution)/shard_map/ppermute | solution.py:233
  68.8 3.0 %collective-permute-start.9 = (bf16[1024,256]{1,0:T(8,128)(2,1)S(1)}, bf16[1024,256]{1,0:T(8,128)(2,1)}, u32[]{:S(2)}, u32[]{:S(2)}) collective-permute-start(bf16[1024,256]{1,0:T(8,128)(2,1)S(1)} %collective-permute-done.5.rest_3_), channel_id=1, source_target_pairs={{0,1},{1,0},{2,3},{3,2},{4,5},{5,4},{6,7},{7,6},{8,9},{9,8},{10,11... | collective-permute-start | bytes 1572872 | tf_op jit(solution)/shard_map/ppermute | solution.py:234
  72.6 1.4 gather_fusion
  74.0 11.2 %all-to-all-start = ((bf16[32,16,512]{2,1,0:T(8,128)(2,1)}), bf16[32,16,512]{2,1,0:T(8,128)(2,1)S(1)}, u32[]{:S(2)}, u32[]{:S(2)}) async-start(bf16[32,16,512]{2,1,0:T(8,128)(2,1)} %gather_fusion), calls=%async_computation | async-start | bytes 1048576 | tf_op jit(solution)/shard_map/all_to_all | solution.py:242
  85.8 1.8 %all-gather.2.cloned.1.call-done.rest_8_ = bf16[4096,512]{1,0:T(8,128)(2,1)} async-done(((bf16[512,512]{1,0:T(8,128)(2,1)}), bf16[4096,512]{1,0:T(8,128)(2,1)}) %all-gather.2.cloned.1.call-update) | async-done | bytes 4194320 | tf_op jit(solution)/shard_map/all_gather | solution.py:229
  87.6 7.9 %shard_map.123 = (f32[256,64]{1,0:T(8,128)}, f32[256,64]{1,0:T(8,128)}, f32[256,512]{1,0:T(8,128)}, bf16[256,512]{1,0:T(8,128)(2,1)}) custom-call(s32[32]{0:T(128)} %pad_add_fusion.where, bf16[32,8192]{1,0:T(8,128)(2,1)} %bitcast.14, bf16[32,8192]{1,0:T(8,128)(2,1)} %bitcast.15, bf16[1024,256]{1,0:T(8,128)(2,1)} %copy-done.4, bf16[1024,256]{1,0:T(8,128)(2,1)} %copy-done.5, ...), custom_call_target="tpu_custom_call" | custom-call | flops 2147483648 | bytes 9437184 | tf_op jit(solution)/shard_map/pallas_call | solution.py:169
  95.5 3.2 %collective-permute-start.11 = (f32[256,64]{1,0:T(8,128)}, f32[256,64]{1,0:T(8,128)S(1)}, u32[]{:S(2)}, u32[]{:S(2)}) collective-permute-start(f32[256,64]{1,0:T(8,128)} %get-tuple-element.16), channel_id=1, source_target_pairs={{0,16},{16,0},{32,48},{48,32},{64,80},{80,64},{96,112},{112,96},{1... | collective-permute-start | bytes 196616 | tf_op jit(solution)/shard_map/ppermute | solution.py:248
  99.3 2.2 %collective-permute-start.10 = (bf16[256,512]{1,0:T(8,128)(2,1)}, bf16[256,512]{1,0:T(8,128)(2,1)S(1)}, u32[]{:S(2)}, u32[]{:S(2)}) collective-permute-start(bf16[256,512]{1,0:T(8,128)(2,1)} %get-tuple-element.14), channel_id=1, source_target_pairs={{0,16},{16,0},{32,48},{48,32},{64,80},{80,64},{96,112},{112,96},{1... | collective-permute-start | bytes 786440 | tf_op jit(solution)/shard_map/ppermute | solution.py:249
  103.4 19.2 %all_gather.7 = bf16[256,512]{0,1:T(8,128)(2,1)S(1)} all-gather(bf16[256,32]{0,1:T(8,128)(2,1)S(1)} %copy.13), channel_id=1, replica_groups=mesh['req'=32,'tp'=16] {'tp'}, dimensions={1}, use_global_device_ids=true | all-gather | bytes 278528 | tf_op jit(solution)/shard_map/all_gather | solution.py:250
  124.4 4.6 %shard_map.124 = (f32[256,512]{1,0:T(8,128)S(1)}, f32[16,512]{1,0:T(8,128)}, f32[16,256]{1,0:T(8,128)S(1)}) custom-call(s32[1]{0:T(128)} %bitcast.source, f32[256,512]{1,0:T(8,128)S(1)} %copy-done.1, bf16[256,512]{1,0:T(8,128)(2,1)S(1)} %collective-permute-done.10.rest, f32[256,512]{1,0:T(8,128)S(1)} %compare_select_fusion.steps, ...), custom_call_target="tpu_custom_call" | custom-call | flops 16777216 | bytes 8388608 | tf_op jit(solution)/shard_map/pallas_call | solution.py:64
  129.0 13.1 %all_to_all.14 = f32[16,1,256]{2,1,0:T(1,128)S(1)} all-to-all(f32[16,1,256]{2,1,0:T(1,128)S(1)} %copy.14), channel_id=1, replica_groups=mesh['req'=32,'tp'=16] {'tp'}, dimensions={0} | all-to-all | bytes 32768 | tf_op jit(solution)/shard_map/all_to_all | solution.py:258
  (54 shorter events, 10.4 us)
Async XLA Ops:
  7.2 115.5 %copy-start = (bf16[512,512]{1,0:T(8,128)(2,1)S(1)}, bf16[512,512]{1,0:T(8,128)(2,1)}, u32[]{:S(2)}) copy-start(bf16[512,512]{1,0:T(8,128)(2,1)} %param.15) | copy-start | bytes 1572868
  7.2 80.4 %all-gather.2.cloned.1.call-start = ((), (), s32[]{:S(2)}) async-start(), calls=%async_computation.2 | async-start | bytes 4718592 | tf_op jit(solution)/shard_map/all_gather | solution.py:229
  7.2 14.4 %collective-permute-start = (bf16[256,512]{1,0:T(8,128)(2,1)}, bf16[256,512]{1,0:T(8,128)(2,1)S(1)}, u32[]{:S(2)}, u32[]{:S(2)}) collective-permute-start(bf16[256,512]{1,0:T(8,128)(2,1)} %weight.1), channel_id=1, source_target_pairs={{0,32},{16,48},{32,0},{48,16},{64,96},{80,112},{96,64},{112,80},{1... | collective-permute-start | bytes 786440 | tf_op jit(solution)/shard_map/ppermute | solution.py:226
  14.5 7.1 %collective-permute-start.1 = (bf16[256,256]{1,0:T(8,128)(2,1)S(1)}, bf16[256,256]{1,0:T(8,128)(2,1)S(1)}, u32[]{:S(2)}, u32[]{:S(2)}) collective-permute-start(bf16[256,256]{1,0:T(8,128)(2,1)S(1)} %get-tuple-element.20), channel_id=1, source_target_pairs={{0,16},{16,0},{32,48},{48,32},{64,80},{80,64},{96,112},{112,96},{1... | collective-permute-start | bytes 393224 | tf_op jit(solution)/shard_map/ppermute | solution.py:226
  24.4 6.3 %collective-permute-start.2 = (bf16[512,256]{1,0:T(8,128)(2,1)}, bf16[512,256]{1,0:T(8,128)(2,1)S(1)}, u32[]{:S(2)}, u32[]{:S(2)}) collective-permute-start(bf16[512,256]{1,0:T(8,128)(2,1)} %get-tuple-element.11), channel_id=1, source_target_pairs={{0,1},{1,0},{2,3},{3,2},{4,5},{5,4},{6,7},{7,6},{8,9},{9,8},{10,11... | collective-permute-start | bytes 786440 | tf_op jit(solution)/shard_map/ppermute | solution.py:231
  30.8 56.8 %copy-start.4 = (bf16[1024,256]{1,0:T(8,128)(2,1)}, bf16[1024,256]{1,0:T(8,128)(2,1)S(1)}, u32[]{:S(2)}) copy-start(bf16[1024,256]{1,0:T(8,128)(2,1)S(1)} %constant_dynamic-update-slice_fusion.rest_0_) | copy-start | bytes 1572868
  30.8 10.2 %collective-permute-start.3 = (bf16[1024,256]{1,0:T(8,128)(2,1)S(1)}, bf16[1024,256]{1,0:T(8,128)(2,1)S(1)}, u32[]{:S(2)}, u32[]{:S(2)}) collective-permute-start(bf16[1024,256]{1,0:T(8,128)(2,1)S(1)} %constant_dynamic-update-slice_fusion.rest_0_), channel_id=1, source_target_pairs={{0,2},{1,15},{2,4},{3,1},{4,6},{5,3},{6,8},{7,5},{8,10},{9,7},{10,... | collective-permute-start | bytes 1572872 | tf_op jit(solution)/shard_map/ppermute | solution.py:233
  41.0 46.6 %copy-start.5 = (bf16[1024,256]{1,0:T(8,128)(2,1)}, bf16[1024,256]{1,0:T(8,128)(2,1)S(1)}, u32[]{:S(2)}) copy-start(bf16[1024,256]{1,0:T(8,128)(2,1)S(1)} %collective-permute-done.3.rest_1_) | copy-start | bytes 1572868
  41.0 10.9 %collective-permute-start.4 = (bf16[1024,256]{1,0:T(8,128)(2,1)S(1)}, bf16[1024,256]{1,0:T(8,128)(2,1)S(1)}, u32[]{:S(2)}, u32[]{:S(2)}) collective-permute-start(bf16[1024,256]{1,0:T(8,128)(2,1)S(1)} %collective-permute-done.3.rest_1_), channel_id=1, source_target_pairs={{0,2},{1,15},{2,4},{3,1},{4,6},{5,3},{6,8},{7,5},{8,10},{9,7},{10,... | collective-permute-start | bytes 1572872 | tf_op jit(solution)/shard_map/ppermute | solution.py:233
  51.9 35.8 %copy-start.6 = (bf16[1024,256]{1,0:T(8,128)(2,1)}, bf16[1024,256]{1,0:T(8,128)(2,1)S(1)}, u32[]{:S(2)}) copy-start(bf16[1024,256]{1,0:T(8,128)(2,1)S(1)} %collective-permute-done.4.rest_2_) | copy-start | bytes 1572868
  51.9 11.5 %collective-permute-start.5 = (bf16[1024,256]{1,0:T(8,128)(2,1)S(1)}, bf16[1024,256]{1,0:T(8,128)(2,1)S(1)}, u32[]{:S(2)}, u32[]{:S(2)}) collective-permute-start(bf16[1024,256]{1,0:T(8,128)(2,1)S(1)} %collective-permute-done.4.rest_2_), channel_id=1, source_target_pairs={{0,2},{1,15},{2,4},{3,1},{4,6},{5,3},{6,8},{7,5},{8,10},{9,7},{10,... | collective-permute-start | bytes 1572872 | tf_op jit(solution)/shard_map/ppermute | solution.py:233
  58.4 27.4 %collective-permute-start.7 = (bf16[1024,256]{1,0:T(8,128)(2,1)S(1)}, bf16[1024,256]{1,0:T(8,128)(2,1)}, u32[]{:S(2)}, u32[]{:S(2)}) collective-permute-start(bf16[1024,256]{1,0:T(8,128)(2,1)S(1)} %collective-permute-done.3.rest_1_), channel_id=1, source_target_pairs={{0,1},{1,0},{2,3},{3,2},{4,5},{5,4},{6,7},{7,6},{8,9},{9,8},{10,11... | collective-permute-start | bytes 1572872 | tf_op jit(solution)/shard_map/ppermute | solution.py:234
  60.6 25.2 %collective-permute-start.8 = (bf16[1024,256]{1,0:T(8,128)(2,1)S(1)}, bf16[1024,256]{1,0:T(8,128)(2,1)}, u32[]{:S(2)}, u32[]{:S(2)}) collective-permute-start(bf16[1024,256]{1,0:T(8,128)(2,1)S(1)} %collective-permute-done.4.rest_2_), channel_id=1, source_target_pairs={{0,1},{1,0},{2,3},{3,2},{4,5},{5,4},{6,7},{7,6},{8,9},{9,8},{10,11... | collective-permute-start | bytes 1572872 | tf_op jit(solution)/shard_map/ppermute | solution.py:234
  63.4 24.2 %copy-start.7 = (bf16[1024,256]{1,0:T(8,128)(2,1)}, bf16[1024,256]{1,0:T(8,128)(2,1)S(1)}, u32[]{:S(2)}) copy-start(bf16[1024,256]{1,0:T(8,128)(2,1)S(1)} %collective-permute-done.5.rest_3_) | copy-start | bytes 1572868
  63.4 22.4 %collective-permute-start.6 = (bf16[1024,256]{1,0:T(8,128)(2,1)S(1)}, bf16[1024,256]{1,0:T(8,128)(2,1)}, u32[]{:S(2)}, u32[]{:S(2)}) collective-permute-start(bf16[1024,256]{1,0:T(8,128)(2,1)S(1)} %collective-permute-done.5.rest_3_), channel_id=1, source_target_pairs={{0,2},{1,15},{2,4},{3,1},{4,6},{5,3},{6,8},{7,5},{8,10},{9,7},{10,... | collective-permute-start | bytes 1572872 | tf_op jit(solution)/shard_map/ppermute | solution.py:233
  68.8 17.0 %collective-permute-start.9 = (bf16[1024,256]{1,0:T(8,128)(2,1)S(1)}, bf16[1024,256]{1,0:T(8,128)(2,1)}, u32[]{:S(2)}, u32[]{:S(2)}) collective-permute-start(bf16[1024,256]{1,0:T(8,128)(2,1)S(1)} %collective-permute-done.5.rest_3_), channel_id=1, source_target_pairs={{0,1},{1,0},{2,3},{3,2},{4,5},{5,4},{6,7},{7,6},{8,9},{9,8},{10,11... | collective-permute-start | bytes 1572872 | tf_op jit(solution)/shard_map/ppermute | solution.py:234
  74.0 49.3 %all-to-all-start = ((bf16[32,16,512]{2,1,0:T(8,128)(2,1)}), bf16[32,16,512]{2,1,0:T(8,128)(2,1)S(1)}, u32[]{:S(2)}, u32[]{:S(2)}) async-start(bf16[32,16,512]{2,1,0:T(8,128)(2,1)} %gather_fusion), calls=%async_computation | async-start | bytes 1048576 | tf_op jit(solution)/shard_map/all_to_all | solution.py:242
  87.6 35.1 %copy-start.11 = (f32[512]{0:T(512)S(1)}, f32[512]{0:T(512)}, u32[]{:S(2)}) copy-start(f32[512]{0:T(512)} %param.16) | copy-start | bytes 6148
  95.5 28.9 %copy-start.1 = (f32[256,512]{1,0:T(8,128)S(1)}, f32[256,512]{1,0:T(8,128)}, u32[]{:S(2)}) copy-start(f32[256,512]{1,0:T(8,128)} %get-tuple-element.13.half) | copy-start | bytes 1572868
  95.5 28.9 %copy-start.2 = (f32[16,512]{1,0:T(8,128)S(1)}, f32[16,512]{1,0:T(8,128)}, u32[]{:S(2)}) copy-start(f32[16,512]{1,0:T(8,128)} %decay.1) | copy-start | bytes 98308
  95.5 28.9 %copy-start.3 = (f32[512]{0:T(512)S(1)}, f32[512]{0:T(512)}, u32[]{:S(2)}) copy-start(f32[512]{0:T(512)} %param.18) | copy-start | bytes 6148
  95.5 6.8 %collective-permute-start.11 = (f32[256,64]{1,0:T(8,128)}, f32[256,64]{1,0:T(8,128)S(1)}, u32[]{:S(2)}, u32[]{:S(2)}) collective-permute-start(f32[256,64]{1,0:T(8,128)} %get-tuple-element.16), channel_id=1, source_target_pairs={{0,16},{16,0},{32,48},{48,32},{64,80},{80,64},{96,112},{112,96},{1... | collective-permute-start | bytes 196616 | tf_op jit(solution)/shard_map/ppermute | solution.py:248
  99.3 23.9 %collective-permute-start.10 = (bf16[256,512]{1,0:T(8,128)(2,1)}, bf16[256,512]{1,0:T(8,128)(2,1)S(1)}, u32[]{:S(2)}, u32[]{:S(2)}) collective-permute-start(bf16[256,512]{1,0:T(8,128)(2,1)} %get-tuple-element.14), channel_id=1, source_target_pairs={{0,16},{16,0},{32,48},{48,32},{64,80},{80,64},{96,112},{112,96},{1... | collective-permute-start | bytes 786440 | tf_op jit(solution)/shard_map/ppermute | solution.py:249
  123.2 18.9 %copy-start.10 = (f32[512]{0:T(512)S(1)}, f32[512]{0:T(512)}, u32[]{:S(2)}) copy-start(f32[512]{0:T(512)} %param.19) | copy-start | bytes 6148
  (2 other events, 1.4 us)
Sparse Core Ops, SparseCore 0:
  24.5 63.0 all-gather.1
